TPU v7x, 256 devices: a whole 4x4x8 slice. The times are simulated.
256 devices in a mesh: patch: 32 (over x, z), freq: 8 (over y, core).
Axes of the slice: x: 4, y: 4, z: 8, core: 2. Of those that a mesh axis runs over, the one named last changes fastest.
Arguments:
- traces: bfloat16 [262144, 2048], P(('patch', 'freq')), may hold values from -6 to 6
- routes: int32 [262144, 1], P(('patch', 'freq')), may hold values from 0 to 31; in each aligned block of 1024 rows (0 to 1023, 1024 to 2047, ...) at most 96 rows name the same one
- cells: int32 [262144], P(('patch', 'freq')), may hold values from 0 to 65535
- band_bins: int32 [16], P('freq'), may hold values from 8 to 1023, as said below
- spectral_weight: float32 [16, 2097152], P('freq', 'patch'), may hold values from 0.1 to 1
Outputs:
- interpolated: float32 [2, 16, 2097152], P(None, 'freq', 'patch')
Inputs may be any that keep to these rules, and one draw needn't show every extreme that they name: `band_bins`: distinct and rising frequency bin numbers; the lowest and the highest bin of the range are always in the band.
All inputs are finite; a program needn't handle non-finite values.
Results may differ from a plain program's by a relative error of at most 0.003.
Values may be sent and summed in bfloat16 or wider, within the bound.
A program may use at most 256 MiB of HBM per device.

v0:
```python
import math

import jax
import jax.numpy as jnp
from jax import lax
from jax.sharding import PartitionSpec as P

SIDE = 16
ITERS = 2


EPS = 1e-06
DAMPING = 0.1


def spectral_table(bins, sample_count):
    sample_index = jnp.arange(sample_count, dtype=jnp.int32)
    phase = bins[:, None] * sample_index[None, :] % sample_count
    angle = 2.0 * math.pi / sample_count * phase.astype(jnp.float32)
    factor = 1.0 / math.sqrt(sample_count)
    return jnp.concatenate([jnp.cos(angle) * factor, -jnp.sin(angle) * factor], 0).astype(
        jnp.bfloat16
    )


def slots_of(targets, n_patch):
    matches = (targets[:, None] == jnp.arange(n_patch, dtype=jnp.int32)[None, :]).astype(jnp.int32)
    before = jnp.cumsum(matches, 0) - matches
    return jnp.sum(before * matches, 1)


def apply_left(matrix, field):
    return jnp.einsum("jk,fkl->fjl", matrix, field, precision=lax.Precision.HIGHEST)


def apply_right(field, matrix):
    return jnp.einsum("fjk,kl->fjl", field, matrix, precision=lax.Precision.HIGHEST)


def transform(real_part, imag_part, kern_real, kern_imag):
    left_real = apply_left(kern_real, real_part) - apply_left(kern_imag, imag_part)
    left_imag = apply_left(kern_real, imag_part) + apply_left(kern_imag, real_part)
    out_real = apply_right(left_real, kern_real) - apply_right(left_imag, kern_imag)
    out_imag = apply_right(left_real, kern_imag) + apply_right(left_imag, kern_real)
    return (out_real, out_imag)


def on_device(traces, routes, cells, band_bins, spectral_weight):
    n_patch = lax.axis_size("patch")
    n_freq = lax.axis_size("freq")
    sample_count = traces.shape[1]
    row_count = traces.shape[0]
    per_freq = band_bins.shape[0]
    capacity = 3 * row_count // n_patch
    all_bins = lax.all_gather(band_bins, "freq", axis=0, tiled=True)
    kernel = spectral_table(all_bins, sample_count)
    freq_total = all_bins.shape[0]
    targets = routes[:, 0]
    spectra = jnp.einsum("kt,rt->kr", kernel, traces, preferred_element_type=jnp.float32)
    spectra = spectra.reshape(2, freq_total, row_count)
    route_keys = jnp.broadcast_to(jnp.stack([targets, cells])[:, None, :], (2, n_freq, row_count))
    spread, spread_keys = (
        lax.all_to_all(spectra, "freq", split_axis=1, concat_axis=2, tiled=True),
        lax.all_to_all(route_keys, "freq", split_axis=1, concat_axis=2, tiled=True),
    )
    target_all = spread_keys[0, 0]
    cell_all = spread_keys[1, 0]
    slot_index = slots_of(target_all, n_patch)
    slot_depth = n_freq * capacity
    buffer = jnp.zeros((2 * per_freq, n_patch, slot_depth), jnp.float32)
    buffer = buffer.at[:, target_all, slot_index].set(spread.reshape(2 * per_freq, -1))
    slot_cells = (
        jnp.full((1, n_patch, slot_depth), -1, jnp.int32)
        .at[0, target_all, slot_index]
        .set(cell_all)
    )
    arrived, arrived_cells = (
        lax.all_to_all(buffer, "patch", split_axis=1, concat_axis=1, tiled=True),
        lax.all_to_all(slot_cells, "patch", split_axis=1, concat_axis=1, tiled=True),
    )
    own_spectra = arrived.reshape(2 * per_freq, -1)
    flat_tags = arrived_cells.reshape(-1)
    cell_count = spectral_weight.shape[1]
    target_cell = jnp.where(flat_tags >= 0, flat_tags, cell_count)
    binned = (
        jnp.zeros((2 * per_freq, cell_count), jnp.float32)
        .at[:, target_cell]
        .add(own_spectra, mode="drop")
    )
    counts = jnp.zeros((cell_count,), jnp.float32).at[target_cell].add(1.0, mode="drop")
    side_square = SIDE * SIDE
    flat_cell = jnp.arange(side_square, dtype=jnp.int32)
    upper = flat_cell // SIDE
    lower = flat_cell % SIDE
    phase = (upper[:, None] * upper[None, :] + lower[:, None] * lower[None, :]) % SIDE
    angle = 2.0 * math.pi / SIDE * phase.astype(jnp.float32)
    kern_real = jnp.cos(angle) / SIDE
    kern_imag = -jnp.sin(angle) / SIDE
    weight = spectral_weight.reshape(per_freq, side_square, side_square)
    counts = counts.reshape(side_square, side_square)
    binned = binned.reshape(2, per_freq, side_square, side_square)

    def forward(real_part, imag_part):
        return transform(real_part, imag_part, kern_real, kern_imag)

    def inverse(real_part, imag_part):
        return transform(real_part, imag_part, kern_real, -kern_imag)

    def column(values):
        return values.reshape(per_freq, 1, 1)

    data_real, data_imag = forward(binned[0], binned[1])
    res_real = weight * data_real
    res_imag = weight * data_imag
    dir_real, dir_imag = (res_real, res_imag)
    est_real = jnp.zeros_like(res_real)
    est_imag = jnp.zeros_like(res_imag)
    norm_now = jnp.sum(res_real * res_real + res_imag * res_imag, axis=(1, 2))
    for step in range(ITERS):
        inner_real, inner_imag = inverse(weight * dir_real, weight * dir_imag)
        back_real, back_imag = forward(counts * inner_real, counts * inner_imag)
        img_real = weight * back_real + DAMPING * dir_real
        img_imag = weight * back_imag + DAMPING * dir_imag
        curvature = jnp.sum(dir_real * img_real + dir_imag * img_imag, axis=(1, 2))
        alpha = column(norm_now / (curvature + EPS))
        est_real = est_real + alpha * dir_real
        est_imag = est_imag + alpha * dir_imag
        res_real = res_real - alpha * img_real
        res_imag = res_imag - alpha * img_imag
        norm_next = jnp.sum(res_real * res_real + res_imag * res_imag, axis=(1, 2))
        ratio = column(norm_next / (norm_now + EPS))
        dir_real = res_real + ratio * dir_real
        dir_imag = res_imag + ratio * dir_imag
        norm_now = norm_next
    model_real, model_imag = inverse(weight * est_real, weight * est_imag)
    return jnp.stack([model_real, model_imag]).reshape(2, per_freq, cell_count)


def solution(mesh):
    return jax.shard_map(
        on_device,
        mesh=mesh,
        in_specs=(
            P(("patch", "freq"), None),
            P(("patch", "freq"), None),
            P(("patch", "freq")),
            P("freq"),
            P("freq", "patch"),
        ),
        out_specs=P(None, "freq", "patch"),
        check_vma=False,
    )
```

profile of v0, /device:TPU:1, one launch (start us, length us, event | category | flops | bytes accessed | tf_op | source)
XLA Modules:
  0.0 591.2 jit_solution(12103979713809565605)
XLA Ops:
  1.4 6.5 %all-to-all-start = ((s32[2,8,1024]{2,0,1:T(2,128)}), s32[2,8,1024]{2,0,1:T(2,128)S(1)}, u32[]{:S(2)}, u32[]{:S(2)}) async-start(s32[2,8,1024]{2,0,1:T(2,128)} %broadcast_in_dim.21), calls=%async_computation | async-start | bytes 131072 | tf_op jit(solution)/shard_map/all_to_all | solution.py:64
  10.7 7.6 %all-reduce = s32[16]{0:T(128)S(1)} all-reduce(s32[16]{0:T(128)S(1)} %dynamic-update-slice), channel_id=1, replica_groups=mesh['patch'=32,'freq'=8] {'freq'}, use_global_device_ids=true, to_apply=%add | all-reduce | flops 16 | bytes 128
  18.9 3.5 fusion.116
  23.2 5.4 all-to-all-start.2
  28.8 9.5 %reduce-window.6 = s32[32,64,128]{2,1,0:T(8,128)S(1)} reduce-window(s32[32,64,128]{2,1,0:T(8,128)S(1)} %fusion.37, s32[]{:T(128)} %constant.78.clone.1), window={size=1x1x128 pad=0_0x0_0x127_0}, to_apply=%region_0.1 | reduce-window | flops 33292288 | bytes 2097156 | tf_op jit(solution)/shard_map/reduce-window
  41.3 31.1 %scatter_custom_fusion.2 = s32[24576]{0:T(1024)} fusion(s32[8192]{0:T(1024)S(1)} %broadcast_select_fusion.1, s32[8192]{0:T(1024)S(1)} %bitcast.264, s32[]{:T(128)} %constant.77.clone.1), kind=kCustom, calls=%fused_computation.201 | custom fusion | bytes 98308
  72.5 10.5 %all-to-all-start.1 = ((s32[1,32,768]{2,0,1:T(1,128)}), s32[1,32,768]{2,0,1:T(1,128)S(1)}, u32[]{:S(2)}, u32[]{:S(2)}) async-start(s32[1,32,768]{2,0,1:T(1,128)} %bitcast.8), calls=%async_computation.1 | async-start | bytes 196608 | tf_op jit(solution)/shard_map/all_to_all | solution.py:79
  83.3 2.7 copy.211
  85.9 26.2 %scatter_custom_fusion.3 = f32[4,24576]{0,1:T(8,128)} fusion(s32[8192]{0:T(1024)S(1)} %broadcast_select_fusion, f32[8192,4]{1,0:T(8,128)} %copy.211, f32[]{:T(128)} %constant.76.clone.1), kind=kCustom, calls=%fused_computation.6 | custom fusion | bytes 393728
  112.1 8.1 %copy.212 = f32[4,32,768]{2,0,1:T(4,128)} copy(f32[4,32,768]{0,2,1:T(8,128)} %bitcast.249) | data formatting | bytes 786432 | tf_op jit(solution)/shard_map/scatter | solution.py:71
  120.2 9.7 %all-to-all-start.3 = ((f32[4,32,768]{2,0,1:T(4,128)}), f32[4,32,768]{2,0,1:T(4,128)S(1)}, u32[]{:S(2)}, u32[]{:S(2)}) async-start(f32[4,32,768]{2,0,1:T(4,128)} %copy.212), calls=%async_computation.3 | async-start | bytes 786432 | tf_op jit(solution)/shard_map/all_to_all | solution.py:78
  130.1 128.5 %scatter_custom_fusion.1 = f32[65536]{0:T(1024)S(1)} fusion(s32[24576]{0:T(1024)S(1)} %bitcast.261, f32[24576]{0:T(1024)S(1)} %broadcast.241, f32[]{:T(128)} %constant.76.clone.1), kind=kCustom, calls=%fused_computation.181 | custom fusion | flops 24576 | bytes 262148 | tf_op jit(solution)/shard_map/scatter-add | solution.py:90
  258.7 6.9 %copy.213 = f32[24576,4]{1,0:T(8,128)} copy(f32[24576,4]{0,1:T(4,128)S(1)} %bitcast.251) | data formatting | bytes 786432 | tf_op jit(solution)/shard_map/reshape | solution.py:81
  265.6 144.1 %scatter_custom_fusion = f32[4,65536]{0,1:T(8,128)} fusion(s32[24576]{0:T(1024)S(1)} %bitcast.262, f32[24576,4]{1,0:T(8,128)} %copy.213, f32[]{:T(128)} %constant.76.clone.1), kind=kCustom, calls=%fused_computation.4 | custom fusion | flops 98304 | bytes 1049088 | tf_op jit(solution)/shard_map/scatter-add | solution.py:88
  409.7 44.4 %fusion.391 = (f32[2,65536]{0,1:T(8,128)}, f32[2,65536]{0,1:T(8,128)}) fusion(f32[4,65536]{0,1:T(8,128)} %scatter_custom_fusion), kind=kLoop, calls=%fused_computation.457 | loop fusion | bytes 2097152 | tf_op jit(solution)/shard_map/slice | solution.py:112
  454.1 18.8 %copy.265 = f32[2,256,256]{2,1,0:T(8,128)S(1)} copy(f32[2,256,256]{0,2,1:T(8,128)} %bitcast.233) | data formatting | bytes 1048576 | tf_op jit(solution)/shard_map/squeeze | solution.py:112
  472.9 19.0 %copy.264 = f32[2,256,256]{2,1,0:T(8,128)S(1)} copy(f32[2,256,256]{0,2,1:T(8,128)} %bitcast.232) | data formatting | bytes 1048576 | tf_op jit(solution)/shard_map/squeeze | solution.py:112
  491.9 1.9 fusion.107
  493.8 1.9 fusion.111
  495.8 1.9 fusion.32
  497.7 1.9 fusion.109
  499.7 2.0 fusion.66
  501.6 1.9 fusion.31
  503.6 2.2 fusion.30
  505.8 2.0 fusion.29
  507.7 2.0 fusion.100
  509.7 2.0 fusion.104
  511.7 2.0 fusion.28
  513.7 2.0 fusion.51
  515.6 2.3 fusion.102
  518.0 2.0 fusion.27
  519.9 2.0 fusion.25
  521.9 1.9 fusion.93
  523.9 2.0 fusion.26
  527.8 2.1 fusion.24
  529.9 1.9 fusion.95
  531.8 2.0 fusion.61
  533.8 1.9 fusion.23
  535.8 2.0 fusion.22
  537.7 2.1 add_reduce_fusion.1
  540.6 2.0 fusion.86
  542.6 2.0 fusion.90
  544.5 2.0 fusion.18
  546.5 1.9 fusion.46
  548.5 1.9 fusion.88
  550.4 2.4 fusion.17
  552.8 2.0 fusion.15
  554.8 1.9 fusion.79
  556.7 2.0 fusion.16
  558.7 1.9 fusion.84
  560.6 1.9 fusion.14
  562.6 1.9 fusion.81
  564.5 2.1 fusion.56
  566.7 2.0 fusion.13
  568.6 2.0 fusion.12
  570.6 2.1 fusion.33
  572.9 1.9 fusion.72
  574.8 2.1 fusion.76
  577.0 1.9 fusion.5
  578.9 1.9 fusion.74
  580.9 1.9 fusion.41
  582.8 1.9 fusion.4
  584.8 1.9 convolution_subtract_fusion
  587.1 1.9 convolution_add_fusion
  (51 shorter events, 13.6 us)
Async XLA Ops:
  0.0 40.7 %copy-start.4 = (s32[3]{0:T(128)S(1)}, s32[3]{0:T(128)}, u32[]{:S(2)}) copy-start(s32[3]{0:T(128)} %constant.97) | copy-start | bytes 40
  0.0 40.9 %copy-start.3 = (s32[3]{0:T(128)S(1)}, s32[3]{0:T(128)}, u32[]{:S(2)}) copy-start(s32[3]{0:T(128)} %constant.100) | copy-start | bytes 40
  0.0 41.1 %copy-start.2 = (s32[2]{0:T(128)S(1)}, s32[2]{0:T(128)}, u32[]{:S(2)}) copy-start(s32[2]{0:T(128)} %constant.106) | copy-start | bytes 28
  0.0 72.3 %copy-start.1 = (s32[2]{0:T(128)S(1)}, s32[2]{0:T(128)}, u32[]{:S(2)}) copy-start(s32[2]{0:T(128)} %constant.103) | copy-start | bytes 28
  1.4 21.8 %all-to-all-start = ((s32[2,8,1024]{2,0,1:T(2,128)}), s32[2,8,1024]{2,0,1:T(2,128)S(1)}, u32[]{:S(2)}, u32[]{:S(2)}) async-start(s32[2,8,1024]{2,0,1:T(2,128)} %broadcast_in_dim.21), calls=%async_computation | async-start | bytes 131072 | tf_op jit(solution)/shard_map/all_to_all | solution.py:64
  23.2 49.3 %all-to-all-start.2 = ((f32[2,16,1024]{2,0,1:T(2,128)}), f32[2,16,1024]{2,0,1:T(2,128)S(1)}, u32[]{:S(2)}, u32[]{:S(2)}) async-start(f32[2,16,1024]{2,0,1:T(2,128)} %copy.209), calls=%async_computation.2 | async-start | bytes 262144 | tf_op jit(solution)/shard_map/all_to_all | solution.py:63
  72.5 47.7 %all-to-all-start.1 = ((s32[1,32,768]{2,0,1:T(1,128)}), s32[1,32,768]{2,0,1:T(1,128)S(1)}, u32[]{:S(2)}, u32[]{:S(2)}) async-start(s32[1,32,768]{2,0,1:T(1,128)} %bitcast.8), calls=%async_computation.1 | async-start | bytes 196608 | tf_op jit(solution)/shard_map/all_to_all | solution.py:79
  120.2 138.5 %all-to-all-start.3 = ((f32[4,32,768]{2,0,1:T(4,128)}), f32[4,32,768]{2,0,1:T(4,128)S(1)}, u32[]{:S(2)}, u32[]{:S(2)}) async-start(f32[4,32,768]{2,0,1:T(4,128)} %copy.212), calls=%async_computation.3 | async-start | bytes 786432 | tf_op jit(solution)/shard_map/all_to_all | solution.py:78
  472.8 30.7 %copy-start = (f32[2,65536]{1,0:T(2,128)S(1)}, f32[2,65536]{1,0:T(2,128)}, u32[]{:S(2)}) copy-start(f32[2,65536]{1,0:T(2,128)} %param.9) | copy-start | bytes 1572868
where the time goes:
time: 600 us; the launch traced here: 591 us
  other arithmetic  288 us (48%)
  local copies, waits for them, and re-layouts  163 us (27%)
  matrix products  98.9 us (16%)
  starting transfers between devices  32.1 us (5%)
  blocking collectives  7.64 us (1%)
    scatter-add x1, other arithmetic, on_device(): binned = jnp.zeros((2 * per_freq, cell_count), jnp.float32).at[:, target_...  144 us
    scatter-add x1, other arithmetic, on_device(): jnp.zeros((cell_count,), jnp.float32).at[target_cell].add(1.0, mode='drop')  128 us
    unnamed x16, local copies, waits for them, and re-layouts  59.5 us
    dot_general x24, matrix products, apply_right(): jnp.einsum('fjk,kl->fjl', field, matrix, precision=lax.Precision.HIGHEST)  47.8 us
    dot_general x24, matrix products, apply_left(): jnp.einsum('jk,fkl->fjl', matrix, field, precision=lax.Precision.HIGHEST)  47.6 us
    slice x1, local copies, waits for them, and re-layouts, on_device(): data_real, data_imag = forward(binned[0], binned[1])  44.4 us
    squeeze x2, local copies, waits for them, and re-layouts, on_device(): data_real, data_imag = forward(binned[0], binned[1])  37.8 us
  transfers between devices with their start and end apart: 4, of which 0 were waited for; matrix products, arithmetic and copies ran while one was open for 37% of the time, Pallas kernels for 0%

commit v1 on v0

v1 whole, which is shorter than its diff:
```python
import functools, math
import jax, jax.numpy as jnp
import ml_dtypes
import numpy as np
from jax import lax
from jax.experimental import pallas as pl
from jax.experimental.pallas import tpu as pltpu
F32=jnp.float32; BF=jnp.bfloat16
NTD=(((1,),(1,)),((),()))

def cosine(phase, n):
    quad = (phase + n // 8) // (n // 4)
    rest = (phase - quad * (n // 4)).astype(F32) * (2.0 * math.pi / n)
    sq = rest * rest
    c = 1.0 + sq * (-0.5 + sq * (1.0/24 + sq * (-1.0/720 + sq * (1.0/40320))))
    s = rest * (1.0 + sq * (-1.0/6 + sq * (1.0/120 + sq * (-1.0/5040))))
    odd = (quad & 1) == 1
    val = jnp.where(odd, s, c)
    neg = ((quad + 1) & 2) == 2
    return jnp.where(neg, -val, val)

def make_basis(bins_ref, nt):
    row = lax.broadcasted_iota(jnp.int32, (32, 128), 0)
    which = (row // 4) * 2 + (row & 1)
    k = jnp.zeros((32, 128), jnp.int32)
    for i in range(16):
        k = jnp.where(which == i, bins_ref[i], k)
    part = (row // 2) & 1
    t = lax.broadcasted_iota(jnp.int32, (32, nt), 1)
    kk = jnp.concatenate([k] * (nt // 128), axis=1)
    pp = jnp.concatenate([part] * (nt // 128), axis=1)
    phase = (kk * t + pp * (nt // 4)) & (nt - 1)
    return (cosine(phase, nt) * (1.0 / math.sqrt(nt))).astype(BF)

def routing(route, cell):
    rows = route.shape[1]
    member = (lax.broadcasted_iota(jnp.int32, (32, rows), 0) == route).astype(F32)
    tri = (lax.broadcasted_iota(jnp.int32, (128, 128), 0) < lax.broadcasted_iota(jnp.int32, (128, 128), 1)).astype(F32).astype(BF)
    pieces = [member[:, 128*i:128*i+128] for i in range(rows // 128)]
    inside = jnp.dot(jnp.concatenate(pieces, axis=0).astype(BF), tri, preferred_element_type=F32)
    offset = jnp.zeros((32, 1), F32)
    before = []
    for i, piece in enumerate(pieces):
        before.append(inside[32*i:32*i+32] + offset)
        offset = offset + jnp.sum(piece, axis=1, keepdims=True)
    rank = jnp.sum(member * jnp.concatenate(before, axis=1), axis=0, keepdims=True).astype(jnp.int32)
    return route * 32 + (rank & 31), rank >> 5

def stack_rows(spectra, third, cell):
    rows = spectra.shape[1]
    out = [jnp.where(third == q, spectra, 0.0) for q in range(3)]
    r = lax.broadcasted_iota(jnp.int32, (32, rows), 0)
    high = ((cell >> 8) + 1).astype(F32)
    low = (cell & 255).astype(F32)
    code = jnp.where((r & 4) == 0, high, low)
    out.append(jnp.where((r >> 3) == third, code, 0.0))
    return jnp.concatenate(out, axis=0).astype(BF)

def one_hot_rows(key):
    rows = key.shape[1]
    return jnp.where(lax.broadcasted_iota(jnp.int32, (1024, rows), 0) == key, 1.0, 0.0).astype(BF)

def write_messages(packed, msg_ref):
    lane = lax.broadcasted_iota(jnp.int32, (32, 128), 1) >> 5
    for cb in range(8):
        groups = [packed[32*g:32*g+32, 128*cb:128*cb+128] for g in range(4)]
        for pm in range(4):
            out = jnp.zeros((32, 128), F32)
            for g in range(4):
                piece = groups[g]
                shift = (32 * (g - pm)) % 128
                if shift:
                    piece = pltpu.roll(piece, shift, 1)
                out = jnp.where(lane == g, piece, out)
            msg_ref[4*cb+pm] = out.astype(BF)

def prepare_kernel(bins_ref, traces_ref, route_ref, cell_ref, msg_ref):
    basis = make_basis(bins_ref, traces_ref.shape[1])
    key, third = routing(route_ref[...], cell_ref[...])
    spectra = lax.dot_general(basis, traces_ref[...], NTD, preferred_element_type=F32)
    stacked = stack_rows(spectra, third, cell_ref[...])
    packed = lax.dot_general(stacked, one_hot_rows(key), NTD, preferred_element_type=F32)
    write_messages(packed, msg_ref)

def regroup_kernel(msg_ref, val_ref, cell_ref):
    lane = lax.broadcasted_iota(jnp.int32, (32, 128), 1) >> 5
    lane8 = lane[:8]
    sub = lax.broadcasted_iota(jnp.int32, (8, 128), 0)
    dense, codes = [], []
    for h in range(8):
        msgs = [msg_ref[4*h+i].astype(F32) for i in range(4)]
        for k in range(3):
            last = pltpu.roll(msgs[3], 96 - 32*k, 1)
            dense.append(jnp.where(lane < 3, msgs[k], last))
            out = msgs[3][8*k:8*k+8]
            for q in range(3):
                out = jnp.where(lane8 == q, pltpu.roll(msgs[k][8*q:8*q+8], 32 + 32*q, 1), out)
            codes.append(out)
    for f in range(8):
        tiles = []
        for pair in range(12):
            a = dense[2*pair][8*(f//2):8*(f//2)+8]
            b = dense[2*pair+1][8*(f//2):8*(f//2)+8]
            if f % 2 == 0:
                b = pltpu.roll(b, 4, 0)
            else:
                a = pltpu.roll(a, 4, 0)
            tiles.append(jnp.where(sub < 4, a, b))
        val_ref[f] = jnp.concatenate(tiles, axis=0).astype(BF)
    out = []
    for cg in range(6):
        t = codes[4*cg]
        for i in range(1, 4):
            t = jnp.where((sub & 3) == i, codes[4*cg+i], t)
        out.append(t)
    cell_ref[...] = jnp.concatenate(out, axis=0).astype(BF)
from jax.sharding import PartitionSpec as P
SIDE=16; ITERS=2; EPS=1e-6; DAMPING=0.1

def kernel_table():
    flat = np.arange(256)
    up, lo = flat // 16, flat % 16
    phase = (up[:, None]*up[None, :] + lo[:, None]*lo[None, :]) % 16
    ang = 2.0*np.pi/16*phase
    kr = np.cos(ang)/16; ki = -np.sin(ang)/16
    a = np.block([[kr, -ki], [ki, kr]])
    b = np.block([[kr, ki], [-ki, kr]])
    def parts(m):
        hi = m.astype(ml_dtypes.bfloat16)
        lo = (m - hi.astype(np.float64)).astype(ml_dtypes.bfloat16)
        return hi, lo
    ah, al = parts(a); bh, bl = parts(b)
    return np.stack([ah, al, bh, bl])

def bin_step(vals, codes, cg, iota, comps=4):
    u = jnp.concatenate([codes[8*cg+i:8*cg+i+1] for i in range(4)], axis=1)
    l = jnp.concatenate([codes[8*cg+4+i:8*cg+5+i] for i in range(4)], axis=1)
    mask = (iota + 1.0) == u
    rhs = jnp.where(iota == l, 1.0, 0.0).astype(BF)
    rows = []
    for c in range(comps):
        v = jnp.concatenate([vals[4*(4*cg+i)+c:4*(4*cg+i)+c+1] for i in range(4)], axis=1)
        rows.append(jnp.where(mask, v, 0.0).astype(BF))
    rows.append(jnp.where(mask, 1.0, 0.0).astype(BF))
    return jnp.concatenate(rows, axis=0), rhs

def split(x):
    hi = x.astype(BF)
    return hi, (x - hi.astype(F32)).astype(BF)

def swap(x):
    return jnp.concatenate([jnp.concatenate([x[:256,:256], x[256:,:256]], axis=1),
                            jnp.concatenate([x[:256,256:], x[256:,256:]], axis=1)], axis=0)

def solve_kernel(val_ref, code_ref, w_ref, tab_ref, out_ref, acc_ref):
    acc_ref[...] = jnp.zeros_like(acc_ref)
    @pl.loop(0, 8)
    def _(g):
        vals = val_ref[g].astype(F32)
        codes = code_ref[g].astype(F32)
        iota = lax.broadcasted_iota(jnp.int32, (256, 512), 0).astype(F32)
        for cg in range(6):
            lhs, rhs = bin_step(vals, codes, cg, iota)
            acc_ref[...] += lax.dot_general(lhs, rhs, NTD, preferred_element_type=F32)
    def left(x, which):
        hi, lo = split(x)
        m, ml = tab_ref[2*which], tab_ref[2*which+1]
        d = functools.partial(jnp.dot, preferred_element_type=F32)
        return d(m, hi) + d(m, lo) + d(ml, hi)
    def right(x, which):
        hi, lo = split(x)
        m, ml = tab_ref[2*which], tab_ref[2*which+1]
        d = functools.partial(jnp.dot, preferred_element_type=F32)
        return d(hi, m) + d(lo, m) + d(hi, ml)
    def forward(x):
        return swap(right(swap(left(x, 0)), 1))
    def inverse(x):
        return swap(right(swap(left(x, 1)), 0))
    def quad(a, b, c, d):
        return jnp.concatenate([jnp.concatenate([a, b], axis=1), jnp.concatenate([c, d], axis=1)], axis=0)
    w = quad(w_ref[0], w_ref[1], w_ref[0], w_ref[1])
    lane = lax.broadcasted_iota(jnp.int32, (1, 512), 1)
    def total(x):
        s = jnp.sum(x, axis=0, keepdims=True)
        a = jnp.sum(s[:, :256], axis=1, keepdims=True)
        b = jnp.sum(s[:, 256:], axis=1, keepdims=True)
        return jnp.where(lane < 256, a, b)
    hits = acc_ref[1024:1280]
    hits = quad(hits, hits, hits, hits)
    field = quad(acc_ref[0:256], acc_ref[256:512], acc_ref[512:768], acc_ref[768:1024])
    residual = w * forward(field)
    direction = residual
    norm = total(residual * residual)
    estimate = None
    for step in range(ITERS):
        image = w * forward(hits * inverse(w * direction)) + DAMPING * direction
        alpha = norm / (total(direction * image) + EPS)
        if step == 0:
            estimate = alpha * direction
        else:
            estimate = estimate + alpha * direction
        if step + 1 < ITERS:
            residual = residual - alpha * image
            new = total(residual * residual)
            direction = residual + (new / (norm + EPS)) * direction
            norm = new
    model = inverse(w * estimate)
    out_ref[0, 0] = model[:256, :256]
    out_ref[0, 1] = model[:256, 256:]
    out_ref[1, 0] = model[256:, :256]
    out_ref[1, 1] = model[256:, 256:]

def on_device(traces, routes, cells, band_bins, spectral_weight):
    n_freq = lax.axis_size("freq")
    rows = traces.shape[0]
    all_bins = lax.all_to_all(jnp.broadcast_to(band_bins[None, :], (n_freq, 2)), "freq", 0, 0, tiled=True).reshape(16)
    vm = pl.BlockSpec(memory_space=pltpu.VMEM)
    params = pltpu.CompilerParams(vmem_limit_bytes=60 * 1024 * 1024)
    msgs = pl.pallas_call(
        prepare_kernel,
        out_shape=jax.ShapeDtypeStruct((32, 32, 128), BF),
        in_specs=[pl.BlockSpec(memory_space=pltpu.SMEM), vm, vm, vm],
        out_specs=vm,
        compiler_params=params,
        name="prepare",
    )(all_bins, traces, routes.reshape(1, rows), cells.reshape(1, rows))
    arrived = lax.all_to_all(msgs, "patch", 0, 0, tiled=True)
    vals, codes = pl.pallas_call(
        regroup_kernel,
        out_shape=[jax.ShapeDtypeStruct((8, 96, 128), BF), jax.ShapeDtypeStruct((48, 128), BF)],
        in_specs=[vm], out_specs=[vm, vm], compiler_params=params,
        name="regroup",
    )(arrived)
    both = jnp.concatenate([vals, jnp.broadcast_to(codes[None], (8, 48, 128))], axis=1)
    both = lax.all_to_all(both, "freq", 0, 0, tiled=True)
    out = pl.pallas_call(
        solve_kernel,
        out_shape=jax.ShapeDtypeStruct((2, 2, 256, 256), F32),
        in_specs=[vm] * 4, out_specs=vm,
        scratch_shapes=[pltpu.VMEM((1280, 256), F32)],
        compiler_params=params,
        name="solve",
    )(both[:, :96], both[:, 96:], spectral_weight.reshape(2, 256, 256), jnp.asarray(kernel_table()))
    return out.reshape(2, 2, 65536)


def solution(mesh):
    return jax.shard_map(
        on_device,
        mesh=mesh,
        in_specs=(P(("patch", "freq"), None), P(("patch", "freq"), None), P(("patch", "freq")), P("freq"), P("freq", "patch")),
        out_specs=P(None, "freq", "patch"),
        check_vma=False,
    )
```

time: 600 us -> 93.3 us (0.16); the launches traced: 591 us -> 92.9 us
  other arithmetic: 288 us -> 2.31 us
  local copies, waits for them, and re-layouts: 163 us -> 7.28 us
  matrix products: 98.9 us -> 0 us
  Pallas kernels: 0 us -> 39 us
  starting transfers between devices: 32.1 us -> 7.05 us
  blocking collectives: 7.64 us -> 31.2 us
    scatter-add x2 -> x0, other arithmetic: 273 us -> none  [the longest x1 144 us: on_device(): binned = jnp.zeros((2 * per_freq, cell_count), jnp.float32).at[:, target_...]
    dot_general x49 -> x0, matrix products: 98.9 us -> none  [the longest x24 47.8 us: apply_right(): jnp.einsum('fjk,kl->fjl', field, matrix, precision=lax.Precision.HIGHEST)]
    unnamed x16 -> x3, local copies, waits for them, and re-layouts: 59.5 us -> 0.84 us
    slice x3 -> x2, local copies, waits for them, and re-layouts: 45.3 us -> 1.33 us  [the longest x1 0.7 us: on_device(): both[:, :96]]
    pallas_call x0 -> x3, Pallas kernels: none -> 39 us  [the longest x1 32.1 us: on_device(): pl.pallas_call(solve_kernel, out_shape=jax.ShapeDtypeStruct((2, 2, 256, 2...]
    squeeze x2 -> x0, local copies, waits for them, and re-layouts: 37.8 us -> none  [on_device(): data_real, data_imag = forward(binned[0], binned[1])]
    all_to_all x0 -> x2, blocking collectives: none -> 31.2 us  [the longest x1 20.8 us: on_device(): arrived = lax.all_to_all(msgs, 'patch', 0, 0, tiled=True)]
    all_to_all x4 -> x1, starting transfers between devices: 32.1 us -> 7.05 us  [on_device(): both = lax.all_to_all(both, 'freq', 0, 0, tiled=True)]
  transfers between devices with their start and end apart: 4 -> 1, of which waited for: 0 -> 1; matrix products, arithmetic and copies ran while one was open for 37% -> 1% of each run, Pallas kernels for 0% -> 0%
where the time goes in v1:
time: 93.3 us; the launch traced here: 92.9 us
  Pallas kernels  39 us (42%)
  blocking collectives  31.2 us (33%)
  local copies, waits for them, and re-layouts  7.28 us (8%)
  starting transfers between devices  7.05 us (8%)
  waiting for transfers between devices  6 us (6%)
  other arithmetic  2.31 us (2%)
    pallas_call x1, Pallas kernels, on_device(): pl.pallas_call(solve_kernel, out_shape=jax.ShapeDtypeStruct((2, 2, 256, 2...  32.1 us
    all_to_all x1, blocking collectives, on_device(): arrived = lax.all_to_all(msgs, 'patch', 0, 0, tiled=True)  20.8 us
    all_to_all x1, blocking collectives, on_device(): lax.all_to_all(jnp.broadcast_to(band_bins[None, :], (n_freq, 2)), 'freq',...  10.3 us
    all_to_all x1, starting transfers between devices, on_device(): both = lax.all_to_all(both, 'freq', 0, 0, tiled=True)  7.05 us
    all_to_all x1, waiting for transfers between devices, on_device(): both = lax.all_to_all(both, 'freq', 0, 0, tiled=True)  6 us
    pallas_call x1, Pallas kernels, on_device(): pl.pallas_call(prepare_kernel, out_shape=jax.ShapeDtypeStruct((32, 32, 12...  5.16 us
    reshape x1, local copies, waits for them, and re-layouts, on_device(): return out.reshape(2, 2, 65536)  2.55 us
  transfers between devices with their start and end apart: 1, of which 1 were waited for; matrix products, arithmetic and copies ran while one was open for 1% of the time, Pallas kernels for 0%

profile of v1, /device:TPU:1, one launch (start us, length us, event | category | flops | bytes accessed | tf_op | source)
XLA Modules:
  0.0 92.9 jit_solution(2061838004987002821)
XLA Ops:
  0.0 0.0 copy-start
  0.0 0.7 broadcast_in_dim.4
  0.7 10.3 %all_to_all.16 = s32[8,1,2]{2,1,0:T(1,128)S(1)} all-to-all(s32[8,1,2]{2,1,0:T(1,128)S(1)} %broadcast_in_dim.4), channel_id=1, replica_groups=mesh['patch'=32,'freq'=8] {'freq'}, dimensions={0} | all-to-all | bytes 128 | tf_op jit(solution)/shard_map/all_to_all | solution.py:216
  11.1 0.5 broadcast.7
  11.6 0.7 reduce.3
  12.2 0.6 reshape.23.bins_ref
  12.8 5.2 %prepare.1 = bf16[32,32,128]{2,1,0:T(8,128)(2,1)} custom-call(s32[16]{0:T(128)} %reshape.23.bins_ref, bf16[1024,2048]{1,0:T(8,128)(2,1)} %traces_ref.1, s32[1,1024]{1,0:T(1,128)} %bitcast.10, s32[1,1024]{1,0:T(1,128)} %bitcast.11), custom_call_target="tpu_custom_call" | custom-call | tf_op jit(solution)/shard_map/prepare/pallas_call | solution.py:219
  18.0 20.8 %all_to_all.17.msg_ref = bf16[32,32,128]{2,1,0:T(8,128)(2,1)} all-to-all(bf16[32,32,128]{2,1,0:T(8,128)(2,1)} %prepare.1), channel_id=1, replica_groups=mesh['patch'=32,'freq'=8] {'patch'}, dimensions={0} | all-to-all | bytes 524288 | tf_op jit(solution)/shard_map/all_to_all | solution.py:227
  38.8 1.8 %regroup.1 = (bf16[8,96,128]{2,1,0:T(8,128)(2,1)}, bf16[48,128]{1,0:T(8,128)(2,1)}) custom-call(bf16[32,32,128]{2,1,0:T(8,128)(2,1)} %all_to_all.17.msg_ref), custom_call_target="tpu_custom_call" | custom-call | tf_op jit(solution)/shard_map/regroup/pallas_call | solution.py:228
  40.6 0.7 broadcast_in_dim.5
  41.3 1.7 %pad_maximum_fusion = bf16[8,144,128]{2,1,0:T(8,128)(2,1)} fusion(bf16[8,48,128]{2,1,0:T(8,128)(2,1)S(1)} %broadcast_in_dim.5, bf16[8,96,128]{2,1,0:T(8,128)(2,1)} %get-tuple-element.7), kind=kLoop, calls=%fused_computation.1 | loop fusion | flops 589824 | bytes 589824 | tf_op jit(solution)/shard_map/concatenate | solution.py:234
  43.0 7.1 %all-to-all-start.2 = ((bf16[8,144,128]{2,1,0:T(8,128)(2,1)}), bf16[8,144,128]{2,1,0:T(8,128)(2,1)S(1)}, u32[]{:S(2)}, u32[]{:S(2)}) async-start(bf16[8,144,128]{2,1,0:T(8,128)(2,1)} %pad_maximum_fusion), calls=%async_computation.2 | async-start | bytes 589824 | tf_op jit(solution)/shard_map/all_to_all | solution.py:235
  50.0 0.0 copy-done
  50.0 0.8 copy.9
  50.9 6.0 %all-to-all-done.2 = bf16[8,144,128]{2,1,0:T(8,128)(2,1)S(1)} async-done(((bf16[8,144,128]{2,1,0:T(8,128)(2,1)}), bf16[8,144,128]{2,1,0:T(8,128)(2,1)S(1)}, u32[]{:S(2)}, u32[]{:S(2)}) %all-to-all-start.2) | async-done | bytes 294944 | tf_op jit(solution)/shard_map/all_to_all | solution.py:235
  56.9 0.6 slice.9.code_ref
  57.5 0.7 slice.8.val_ref
  58.2 32.1 %solve.1 = f32[2,2,256,256]{3,2,1,0:T(8,128)} custom-call(bf16[8,96,128]{2,1,0:T(8,128)(2,1)} %slice.8.val_ref, bf16[8,48,128]{2,1,0:T(8,128)(2,1)} %slice.9.code_ref, f32[2,256,256]{2,1,0:T(8,128)} %bitcast.8, bf16[4,512,512]{2,1,0:T(8,128)(2,1)} %constant.2.clone.tab_ref), custom_call_target="tpu_custom_call" | custom-call | tf_op jit(solution)/shard_map/solve/pallas_call | solution.py:236
  90.3 2.6 %reshape.27 = f32[2,2,65536]{2,1,0:T(2,128)} reshape(f32[2,2,256,256]{3,2,1,0:T(8,128)} %solve.1) | data formatting | bytes 2097152 | tf_op jit(solution)/shard_map/reshape | solution.py:244
Async XLA Ops:
  0.0 50.0 %copy-start = (f32[2,65536]{1,0:T(2,128)S(1)}, f32[2,65536]{1,0:T(2,128)}, u32[]{:S(2)}) copy-start(f32[2,65536]{1,0:T(2,128)} %param.10) | copy-start | bytes 1572868
  43.0 13.9 %all-to-all-start.2 = ((bf16[8,144,128]{2,1,0:T(8,128)(2,1)}), bf16[8,144,128]{2,1,0:T(8,128)(2,1)S(1)}, u32[]{:S(2)}, u32[]{:S(2)}) async-start(bf16[8,144,128]{2,1,0:T(8,128)(2,1)} %pad_maximum_fusion), calls=%async_computation.2 | async-start | bytes 589824 | tf_op jit(solution)/shard_map/all_to_all | solution.py:235

commit v2 on v1

--- a/solution.py
+++ b/solution.py
@@ -1,12 +1,13 @@
 import functools, math
-import jax, jax.numpy as jnp
-import ml_dtypes
+import jax
+import jax.numpy as jnp
 import numpy as np
 from jax import lax
 from jax.experimental import pallas as pl
 from jax.experimental.pallas import tpu as pltpu
 F32=jnp.float32; BF=jnp.bfloat16
 NTD=(((1,),(1,)),((),()))
+
 
 def cosine(phase, n):
     quad = (phase + n // 8) // (n // 4)
@@ -20,16 +21,13 @@
     return jnp.where(neg, -val, val)
 
 def make_basis(bins_ref, nt):
-    row = lax.broadcasted_iota(jnp.int32, (32, 128), 0)
-    which = (row // 4) * 2 + (row & 1)
-    k = jnp.zeros((32, 128), jnp.int32)
-    for i in range(16):
-        k = jnp.where(which == i, bins_ref[i], k)
-    part = (row // 2) & 1
+    sub = lax.broadcasted_iota(jnp.int32, (8, 128), 0)
+    k = jnp.concatenate([jnp.where(sub < 4, bins_ref[2 * i], bins_ref[2 * i + 1]) for i in range(4)], axis=0)
+    part = (lax.broadcasted_iota(jnp.int32, (32, 128), 0) // 2) & 1
     t = lax.broadcasted_iota(jnp.int32, (32, nt), 1)
     kk = jnp.concatenate([k] * (nt // 128), axis=1)
-    pp = jnp.concatenate([part] * (nt // 128), axis=1)
-    phase = (kk * t + pp * (nt // 4)) & (nt - 1)
+    pp = jnp.concatenate([part * (nt // 4)] * (nt // 128), axis=1)
+    phase = (kk * t + pp) & (nt - 1)
     return (cosine(phase, nt) * (1.0 / math.sqrt(nt))).astype(BF)
 
 def routing(route, cell):
@@ -74,15 +72,7 @@
                 out = jnp.where(lane == g, piece, out)
             msg_ref[4*cb+pm] = out.astype(BF)
 
-def prepare_kernel(bins_ref, traces_ref, route_ref, cell_ref, msg_ref):
-    basis = make_basis(bins_ref, traces_ref.shape[1])
-    key, third = routing(route_ref[...], cell_ref[...])
-    spectra = lax.dot_general(basis, traces_ref[...], NTD, preferred_element_type=F32)
-    stacked = stack_rows(spectra, third, cell_ref[...])
-    packed = lax.dot_general(stacked, one_hot_rows(key), NTD, preferred_element_type=F32)
-    write_messages(packed, msg_ref)
-
-def regroup_kernel(msg_ref, val_ref, cell_ref):
+def regroup(msg_ref, pair_ref):
     lane = lax.broadcasted_iota(jnp.int32, (32, 128), 1) >> 5
     lane8 = lane[:8]
     sub = lax.broadcasted_iota(jnp.int32, (8, 128), 0)
@@ -106,31 +96,25 @@
             else:
                 a = pltpu.roll(a, 4, 0)
             tiles.append(jnp.where(sub < 4, a, b))
-        val_ref[f] = jnp.concatenate(tiles, axis=0).astype(BF)
+        pair_ref[f, 0:96, :] = jnp.concatenate(tiles, axis=0).astype(BF)
     out = []
     for cg in range(6):
         t = codes[4*cg]
         for i in range(1, 4):
             t = jnp.where((sub & 3) == i, codes[4*cg+i], t)
         out.append(t)
-    cell_ref[...] = jnp.concatenate(out, axis=0).astype(BF)
+    out = jnp.concatenate(out, axis=0).astype(BF)
+    for f in range(8):
+        pair_ref[f, 96:144, :] = out
 from jax.sharding import PartitionSpec as P
 SIDE=16; ITERS=2; EPS=1e-6; DAMPING=0.1
 
 def kernel_table():
     flat = np.arange(256)
-    up, lo = flat // 16, flat % 16
-    phase = (up[:, None]*up[None, :] + lo[:, None]*lo[None, :]) % 16
-    ang = 2.0*np.pi/16*phase
-    kr = np.cos(ang)/16; ki = -np.sin(ang)/16
-    a = np.block([[kr, -ki], [ki, kr]])
-    b = np.block([[kr, ki], [-ki, kr]])
-    def parts(m):
-        hi = m.astype(ml_dtypes.bfloat16)
-        lo = (m - hi.astype(np.float64)).astype(ml_dtypes.bfloat16)
-        return hi, lo
-    ah, al = parts(a); bh, bl = parts(b)
-    return np.stack([ah, al, bh, bl])
+    up, lo = flat // SIDE, flat % SIDE
+    phase = (up[:, None] * up[None, :] + lo[:, None] * lo[None, :]) % SIDE
+    angle = 2.0 * np.pi / SIDE * phase
+    return np.stack([np.cos(angle) / SIDE, -np.sin(angle) / SIDE]).astype(np.float32)
 
 def bin_step(vals, codes, cg, iota, comps=4):
     u = jnp.concatenate([codes[8*cg+i:8*cg+i+1] for i in range(4)], axis=1)
@@ -152,33 +136,44 @@
     return jnp.concatenate([jnp.concatenate([x[:256,:256], x[256:,:256]], axis=1),
                             jnp.concatenate([x[:256,256:], x[256:,256:]], axis=1)], axis=0)
 
-def solve_kernel(val_ref, code_ref, w_ref, tab_ref, out_ref, acc_ref):
+def solve_kernel(pair_ref, w_ref, tab_ref, out_ref, acc_ref):
     acc_ref[...] = jnp.zeros_like(acc_ref)
     @pl.loop(0, 8)
     def _(g):
-        vals = val_ref[g].astype(F32)
-        codes = code_ref[g].astype(F32)
+        vals = pair_ref[g, 0:96, :].astype(F32)
+        codes = pair_ref[g, 96:144, :].astype(F32)
         iota = lax.broadcasted_iota(jnp.int32, (256, 512), 0).astype(F32)
         for cg in range(6):
             lhs, rhs = bin_step(vals, codes, cg, iota)
             acc_ref[...] += lax.dot_general(lhs, rhs, NTD, preferred_element_type=F32)
+    kr, krl = split(tab_ref[0])
+    ki, kil = split(tab_ref[1])
+
+    def quad(a, b, c, d):
+        return jnp.concatenate([jnp.concatenate([a, b], axis=1), jnp.concatenate([c, d], axis=1)], axis=0)
+
+    tables = (quad(kr, -ki, ki, kr), quad(krl, -kil, kil, krl), quad(kr, ki, -ki, kr), quad(krl, kil, -kil, krl))
+    dot = functools.partial(jnp.dot, preferred_element_type=F32)
+
     def left(x, which):
         hi, lo = split(x)
-        m, ml = tab_ref[2*which], tab_ref[2*which+1]
-        d = functools.partial(jnp.dot, preferred_element_type=F32)
-        return d(m, hi) + d(m, lo) + d(ml, hi)
+        m, ml = tables[2 * which], tables[2 * which + 1]
+        return dot(m, hi) + dot(m, lo) + dot(ml, hi)
+
     def right(x, which):
         hi, lo = split(x)
-        m, ml = tab_ref[2*which], tab_ref[2*which+1]
-        d = functools.partial(jnp.dot, preferred_element_type=F32)
-        return d(hi, m) + d(lo, m) + d(hi, ml)
+        m, ml = tables[2 * which], tables[2 * which + 1]
+        return dot(hi, m) + dot(lo, m) + dot(hi, ml)
+
     def forward(x):
         return swap(right(swap(left(x, 0)), 1))
     def inverse(x):
         return swap(right(swap(left(x, 1)), 0))
-    def quad(a, b, c, d):
-        return jnp.concatenate([jnp.concatenate([a, b], axis=1), jnp.concatenate([c, d], axis=1)], axis=0)
-    w = quad(w_ref[0], w_ref[1], w_ref[0], w_ref[1])
+    def plane(f):
+        return jnp.concatenate([w_ref[pl.ds(2 * h + f, 256, stride=4), :] for h in range(2)], axis=1)
+
+    w0, w1 = plane(0), plane(1)
+    w = quad(w0, w1, w0, w1)
     lane = lax.broadcasted_iota(jnp.int32, (1, 512), 1)
     def total(x):
         s = jnp.sum(x, axis=0, keepdims=True)
@@ -205,43 +200,98 @@
             direction = residual + (new / (norm + EPS)) * direction
             norm = new
     model = inverse(w * estimate)
-    out_ref[0, 0] = model[:256, :256]
-    out_ref[0, 1] = model[:256, 256:]
-    out_ref[1, 0] = model[256:, :256]
-    out_ref[1, 1] = model[256:, 256:]
+    for part in range(2):
+        for f in range(2):
+            for h in range(2):
+                out_ref[part, pl.ds(2 * h + f, 256, stride=4), :] = model[256 * part:256 * part + 256, 256 * f + 128 * h:256 * f + 128 * h + 128]
+
+
+def peer_loop(n, me, body):
+    lax.fori_loop(1, n, lambda i, carry: (body(lax.rem(me + i, n)), carry)[1], 0)
+
+
+def exchange_kernel(bins_ref, traces_ref, route_ref, cell_ref, out_ref,
+                    traces_vm, hot_vm, bins_vm, msg_out, msg_in, pair_out,
+                    trace_sem, bin_send, bin_recv, msg_send, msg_recv, pair_send, pair_recv):
+    me_p, me_f = lax.axis_index("patch"), lax.axis_index("freq")
+    barrier = pltpu.get_barrier_semaphore()
+    mesh_id = pl.DeviceIdType.MESH
+    peer_loop(8, me_f, lambda f: pl.semaphore_signal(barrier, inc=1, device_id={"freq": f}, device_id_type=mesh_id))
+    peer_loop(32, me_p, lambda p: pl.semaphore_signal(barrier, inc=1, device_id={"patch": p}, device_id_type=mesh_id))
+    fetch = pltpu.make_async_copy(traces_ref, traces_vm, trace_sem)
+    fetch.start()
+    sub = lax.broadcasted_iota(jnp.int32, (8, 128), 0)
+    bins_vm[me_f] = jnp.where((sub & 1) == 1, bins_ref[1], bins_ref[0])
+    key, third = routing(route_ref[...], cell_ref[...])
+    hot_vm[...] = one_hot_rows(key)
+    pl.semaphore_wait(barrier, 38)
+
+    def bin_copy(f, slot):
+        return pltpu.make_async_remote_copy(
+            src_ref=bins_vm.at[me_f], dst_ref=bins_vm.at[slot], send_sem=bin_send.at[f],
+            recv_sem=bin_recv.at[slot], device_id={"freq": f}, device_id_type=mesh_id)
+
+    def msg_copy(p, slot):
+        return pltpu.make_async_remote_copy(
+            src_ref=msg_out.at[p], dst_ref=msg_in.at[slot], send_sem=msg_send.at[p],
+            recv_sem=msg_recv.at[slot], device_id={"patch": p}, device_id_type=mesh_id)
+
+    def pair_copy(f, slot):
+        return pltpu.make_async_remote_copy(
+            src_ref=pair_out.at[f], dst_ref=out_ref.at[slot], send_sem=pair_send.at[f],
+            recv_sem=pair_recv.at[slot], device_id={"freq": f}, device_id_type=mesh_id)
+
+    peer_loop(8, me_f, lambda f: bin_copy(f, me_f).start())
+    peer_loop(8, me_f, lambda f: bin_copy(f, f).wait_recv())
+    basis = make_basis(bins_vm, traces_vm.shape[1])
+    fetch.wait()
+    spectra = lax.dot_general(basis, traces_vm[...], NTD, preferred_element_type=F32)
+    stacked = stack_rows(spectra, third, cell_ref[...])
+    packed = lax.dot_general(stacked, hot_vm[...], NTD, preferred_element_type=F32)
+    write_messages(packed, msg_out)
+    peer_loop(32, me_p, lambda p: msg_copy(p, me_p).start())
+    msg_in[me_p] = msg_out[me_p]
+    peer_loop(32, me_p, lambda p: msg_copy(p, p).wait_recv())
+    regroup(msg_in, pair_out)
+    peer_loop(8, me_f, lambda f: pair_copy(f, me_f).start())
+    own = pltpu.make_async_copy(pair_out.at[me_f], out_ref.at[me_f], trace_sem)
+    own.start()
+    peer_loop(8, me_f, lambda f: bin_copy(f, me_f).wait_send())
+    peer_loop(32, me_p, lambda p: msg_copy(p, me_p).wait_send())
+    own.wait()
+    peer_loop(8, me_f, lambda f: pair_copy(f, f).wait_recv())
+    peer_loop(8, me_f, lambda f: pair_copy(f, me_f).wait_send())
 
 def on_device(traces, routes, cells, band_bins, spectral_weight):
-    n_freq = lax.axis_size("freq")
     rows = traces.shape[0]
-    all_bins = lax.all_to_all(jnp.broadcast_to(band_bins[None, :], (n_freq, 2)), "freq", 0, 0, tiled=True).reshape(16)
     vm = pl.BlockSpec(memory_space=pltpu.VMEM)
-    params = pltpu.CompilerParams(vmem_limit_bytes=60 * 1024 * 1024)
-    msgs = pl.pallas_call(
-        prepare_kernel,
-        out_shape=jax.ShapeDtypeStruct((32, 32, 128), BF),
-        in_specs=[pl.BlockSpec(memory_space=pltpu.SMEM), vm, vm, vm],
-        out_specs=vm,
-        compiler_params=params,
-        name="prepare",
-    )(all_bins, traces, routes.reshape(1, rows), cells.reshape(1, rows))
-    arrived = lax.all_to_all(msgs, "patch", 0, 0, tiled=True)
-    vals, codes = pl.pallas_call(
-        regroup_kernel,
-        out_shape=[jax.ShapeDtypeStruct((8, 96, 128), BF), jax.ShapeDtypeStruct((48, 128), BF)],
-        in_specs=[vm], out_specs=[vm, vm], compiler_params=params,
-        name="regroup",
-    )(arrived)
-    both = jnp.concatenate([vals, jnp.broadcast_to(codes[None], (8, 48, 128))], axis=1)
-    both = lax.all_to_all(both, "freq", 0, 0, tiled=True)
+    sm = pl.BlockSpec(memory_space=pltpu.SMEM)
+    anywhere = pl.BlockSpec(memory_space=pl.ANY)
+    dma = pltpu.SemaphoreType.DMA
+    both = pl.pallas_call(
+        exchange_kernel,
+        out_shape=jax.ShapeDtypeStruct((8, 144, 128), BF),
+        in_specs=[sm, anywhere, vm, vm],
+        out_specs=anywhere,
+        scratch_shapes=[
+            pltpu.VMEM(traces.shape, BF), pltpu.VMEM((1024, rows), BF), pltpu.VMEM((8, 8, 128), jnp.int32),
+            pltpu.VMEM((32, 32, 128), BF), pltpu.VMEM((32, 32, 128), BF), pltpu.VMEM((8, 144, 128), BF),
+            dma, dma((8,)), dma((8,)), dma((32,)), dma((32,)), dma((8,)), dma((8,)),
+        ],
+        compiler_params=pltpu.CompilerParams(
+            collective_id=0, has_side_effects=True, vmem_limit_bytes=48 * 1024 * 1024),
+        name="exchange",
+    )(band_bins, traces, routes.reshape(1, rows), cells.reshape(1, rows))
+    weight = spectral_weight.reshape(2, 512, 128).transpose(1, 0, 2).reshape(1024, 128)
     out = pl.pallas_call(
         solve_kernel,
-        out_shape=jax.ShapeDtypeStruct((2, 2, 256, 256), F32),
-        in_specs=[vm] * 4, out_specs=vm,
+        out_shape=jax.ShapeDtypeStruct((2, 1024, 128), F32),
+        in_specs=[vm] * 3, out_specs=vm,
         scratch_shapes=[pltpu.VMEM((1280, 256), F32)],
-        compiler_params=params,
+        compiler_params=pltpu.CompilerParams(vmem_limit_bytes=60 * 1024 * 1024),
         name="solve",
-    )(both[:, :96], both[:, 96:], spectral_weight.reshape(2, 256, 256), jnp.asarray(kernel_table()))
-    return out.reshape(2, 2, 65536)
+    )(both, weight, jnp.asarray(kernel_table()))
+    return out.reshape(2, 512, 2, 128).transpose(0, 2, 1, 3).reshape(2, 2, 65536)
 
 
 def solution(mesh):

time: 93.3 us -> 69.8 us (0.75)
  blocking collectives: 31.2 us -> 0 us
  Pallas kernels: 39 us -> 64.7 us
  starting transfers between devices: 7.05 us -> 0 us
  waiting for transfers between devices: 6 us -> 0 us
  local copies, waits for them, and re-layouts: 7.28 us -> 4.92 us
  other arithmetic: 2.31 us -> 0 us
    all_to_all x2 -> x0, blocking collectives: 31.2 us -> none  [the longest x1 20.8 us: on_device(): arrived = lax.all_to_all(msgs, 'patch', 0, 0, tiled=True)]
    pallas_call x3 -> x2, Pallas kernels: 39 us -> 64.7 us  [the longest x1 33 us: on_device(): pl.pallas_call(exchange_kernel, out_shape=jax.ShapeDtypeStruct((8, 144, 1...]
    all_to_all x1 -> x0, starting transfers between devices: 7.05 us -> none  [on_device(): both = lax.all_to_all(both, 'freq', 0, 0, tiled=True)]
    all_to_all x1 -> x0, waiting for transfers between devices: 6 us -> none  [on_device(): both = lax.all_to_all(both, 'freq', 0, 0, tiled=True)]
    unnamed x3 -> x10, local copies, waits for them, and re-layouts: 0.84 us -> 4.92 us
    reshape x2 -> x0, local copies, waits for them, and re-layouts: 3.17 us -> none  [the longest x1 2.55 us: on_device(): return out.reshape(2, 2, 65536)]
    concatenate x1 -> x0, other arithmetic: 1.65 us -> none  [on_device(): jnp.concatenate([vals, jnp.broadcast_to(codes[None], (8, 48, 128))], axis=1)]
    broadcast_in_dim x2 -> x0, local copies, waits for them, and re-layouts: 1.44 us -> none  [the longest x1 0.72 us: on_device(): jnp.broadcast_to(codes[None], (8, 48, 128))]
  transfers between devices with their start and end apart: 1 -> 0, of which waited for: 1 -> 0; matrix products, arithmetic and copies ran while one was open for 1% -> 0% of each run, Pallas kernels for 0% -> 0%
where the time goes in v2:
time: 69.8 us; the launch traced here: 69.6 us
  Pallas kernels  64.7 us (93%)
  local copies, waits for them, and re-layouts  4.92 us (7%)
    pallas_call x1, Pallas kernels, on_device(): pl.pallas_call(exchange_kernel, out_shape=jax.ShapeDtypeStruct((8, 144, 1...  33 us
    pallas_call x1, Pallas kernels, on_device(): pl.pallas_call(solve_kernel, out_shape=jax.ShapeDtypeStruct((2, 1024, 128...  31.7 us
    unnamed x10, local copies, waits for them, and re-layouts  4.92 us

profile of v2, /device:TPU:1, one launch (start us, length us, event | category | flops | bytes accessed | tf_op | source)
XLA Modules:
  0.0 69.6 jit_solution(6718689330401049669)
XLA Ops:
  0.0 0.0 copy-start
  0.0 2.2 %copy-done = bf16[1024,2048]{1,0:T(8,128)(2,1)S(1)} copy-done((bf16[1024,2048]{1,0:T(8,128)(2,1)S(1)}, bf16[1024,2048]{1,0:T(8,128)(2,1)}, u32[]{:S(2)}) %copy-start) | copy-done | bytes 4194328
  2.2 0.0 copy-start.2
  2.2 0.7 copy-done.2
  2.9 0.0 copy-start.3
  2.9 0.7 copy-done.3
  3.6 0.0 copy-start.4
  3.6 0.7 copy-done.4
  4.2 33.0 %exchange.1.pair_ref = bf16[8,144,128]{2,1,0:T(8,128)(2,1)S(1)} custom-call(s32[2]{0:T(128)S(1)} %copy-done.4, bf16[1024,2048]{1,0:T(8,128)(2,1)S(1)} %copy-done, s32[1,1024]{1,0:T(1,128)S(1)} %bitcast.12, s32[1,1024]{1,0:T(1,128)S(1)} %bitcast.13), custom_call_target="tpu_custom_call" | custom-call | tf_op jit(solution)/shard_map/exchange/pallas_call | solution.py:271
  37.2 0.0 copy-start.1
  37.2 0.7 %copy-done.1 = bf16[8,144,128]{2,1,0:T(8,128)(2,1)} copy-done((bf16[8,144,128]{2,1,0:T(8,128)(2,1)}, bf16[8,144,128]{2,1,0:T(8,128)(2,1)S(1)}, u32[]{:S(2)}) %copy-start.1) | copy-done | bytes 294936
  37.9 31.7 %solve.1 = f32[2,1024,128]{2,1,0:T(8,128)} custom-call(bf16[8,144,128]{2,1,0:T(8,128)(2,1)} %copy-done.1, f32[1024,128]{1,0:T(8,128)} %bitcast.14, f32[2,256,256]{2,1,0:T(8,128)} %constant.2.clone.tab_ref), custom_call_target="tpu_custom_call" | custom-call | tf_op jit(solution)/shard_map/solve/pallas_call | solution.py:286
Async XLA Ops:
  0.0 2.2 %copy-start = (bf16[1024,2048]{1,0:T(8,128)(2,1)S(1)}, bf16[1024,2048]{1,0:T(8,128)(2,1)}, u32[]{:S(2)}) copy-start(bf16[1024,2048]{1,0:T(8,128)(2,1)} %traces_ref.1) | copy-start | bytes 12582916
  2.2 0.7 copy-start.2
  2.9 0.7 copy-start.3
  3.6 0.7 copy-start.4
  37.2 0.7 %copy-start.1 = (bf16[8,144,128]{2,1,0:T(8,128)(2,1)}, bf16[8,144,128]{2,1,0:T(8,128)(2,1)S(1)}, u32[]{:S(2)}) copy-start(bf16[8,144,128]{2,1,0:T(8,128)(2,1)S(1)} %exchange.1.pair_ref) | copy-start | bytes 884740

commit v3 on v2

v3 whole, which is shorter than its diff:
```python
import functools, math
import jax
import jax.numpy as jnp
import ml_dtypes
import numpy as np
from jax import lax
from jax.experimental import pallas as pl
from jax.experimental.pallas import tpu as pltpu
F32=jnp.float32; BF=jnp.bfloat16
NTD=(((1,),(1,)),((),()))


def cosine(phase, n):
    quad = (phase + n // 8) // (n // 4)
    rest = (phase - quad * (n // 4)).astype(F32) * (2.0 * math.pi / n)
    sq = rest * rest
    c = 1.0 + sq * (-0.5 + sq * (1.0/24 + sq * (-1.0/720 + sq * (1.0/40320))))
    s = rest * (1.0 + sq * (-1.0/6 + sq * (1.0/120 + sq * (-1.0/5040))))
    odd = (quad & 1) == 1
    val = jnp.where(odd, s, c)
    neg = ((quad + 1) & 2) == 2
    return jnp.where(neg, -val, val)

def make_basis(bins_ref, nt):
    sub = lax.broadcasted_iota(jnp.int32, (8, 128), 0)
    k = jnp.concatenate([jnp.where(sub < 4, bins_ref[2 * i], bins_ref[2 * i + 1]) for i in range(4)], axis=0)
    part = (lax.broadcasted_iota(jnp.int32, (32, 128), 0) // 2) & 1
    t = lax.broadcasted_iota(jnp.int32, (32, nt), 1)
    kk = jnp.concatenate([k] * (nt // 128), axis=1)
    pp = jnp.concatenate([part * (nt // 4)] * (nt // 128), axis=1)
    phase = (kk * t + pp) & (nt - 1)
    return (cosine(phase, nt) * (1.0 / math.sqrt(nt))).astype(BF)

def routing(route, cell):
    rows = route.shape[1]
    key = (route << 26) + (cell << 10) + lax.broadcasted_iota(jnp.int32, (1, rows), 1)
    smaller = jnp.zeros((8, rows), F32)
    for a in range(rows // 128):
        column = jnp.broadcast_to(key[:, 128 * a:128 * a + 128], (128, 128)).T
        for i in range(16):
            part = jnp.concatenate([column[8 * i:8 * i + 8]] * (rows // 128), axis=1)
            smaller = smaller + jnp.where(part < key, 1.0, 0.0)
    patch = lax.broadcasted_iota(jnp.int32, (32, rows), 0)
    before = jnp.sum(jnp.where(route < patch, 1.0, 0.0), axis=1, keepdims=True)
    rank = jnp.sum(smaller, axis=0, keepdims=True) - jnp.sum(jnp.where(route == patch, before, 0.0), axis=0, keepdims=True)
    rank = rank.astype(jnp.int32)
    return route * 32 + (rank & 31), rank >> 5

def stack_rows(spectra, third, cell):
    rows = spectra.shape[1]
    out = [jnp.where(third == q, spectra, 0.0) for q in range(3)]
    r = lax.broadcasted_iota(jnp.int32, (32, rows), 0)
    high = ((cell >> 8) + 1).astype(F32)
    low = (cell & 255).astype(F32)
    code = jnp.where((r & 4) == 0, high, low)
    out.append(jnp.where((r >> 3) == third, code, 0.0))
    return jnp.concatenate(out, axis=0).astype(BF)

def one_hot_rows(key):
    rows = key.shape[1]
    return jnp.where(lax.broadcasted_iota(jnp.int32, (1024, rows), 0) == key, 1.0, 0.0).astype(BF)

def write_messages(packed, turn, msg_ref):
    lane = lax.broadcasted_iota(jnp.int32, (32, 128), 1) >> 5
    for cb in range(8):
        groups = [packed[32*g:32*g+32, 128*cb:128*cb+128] for g in range(4)]
        for pm in range(4):
            out = jnp.zeros((32, 128), F32)
            for g in range(4):
                piece = groups[g]
                shift = (32 * (g - pm)) % 128
                if shift:
                    piece = pltpu.roll(piece, shift, 1)
                out = jnp.where(lane == g, piece, out)
            msg_ref[4*cb+pm] = pltpu.roll(out, turn, 1).astype(BF)

def regroup(msg_ref, sources, pair_ref):
    lane = lax.broadcasted_iota(jnp.int32, (32, 128), 1) >> 3
    lane8 = lane[:8]
    sub = lax.broadcasted_iota(jnp.int32, (8, 128), 0)
    msgs = [msg_ref[sources[t]].astype(F32) for t in range(16)]
    dense, codes = [], []
    for b in range(12):
        q = b // 4
        value, code = msgs[0], msgs[0][8 * q:8 * q + 8]
        for t in range(1, 16):
            value = jnp.where(lane == (b + t) % 16, msgs[t], value)
            code = jnp.where(lane8 == (12 + b % 4 + t) % 16, msgs[t][8 * q:8 * q + 8], code)
        dense.append(value)
        codes.append(pltpu.roll(code, 32 + 32 * q, 1))
    for f in range(8):
        tiles = []
        for pair in range(6):
            a = dense[2 * pair][8 * (f // 2):8 * (f // 2) + 8]
            b = dense[2 * pair + 1][8 * (f // 2):8 * (f // 2) + 8]
            if f % 2 == 0:
                b = pltpu.roll(b, 4, 0)
            else:
                a = pltpu.roll(a, 4, 0)
            tiles.append(jnp.where(sub < 4, a, b))
        pair_ref[f, 0:48, :] = jnp.concatenate(tiles, axis=0).astype(BF)
    out = []
    for cg in range(3):
        t = codes[4 * cg]
        for i in range(1, 4):
            t = jnp.where((sub & 3) == i, codes[4 * cg + i], t)
        out.append(t)
    out = jnp.concatenate(out, axis=0).astype(BF)
    for f in range(8):
        pair_ref[f, 48:72, :] = out
from jax.sharding import PartitionSpec as P
SIDE = 16
EPS = 1e-6
DAMPING = 0.1
STRETCH = 1.135235
CENTER = 0.99785729


def kernel_table():
    flat = np.arange(256)
    up, lo = flat // SIDE, flat % SIDE
    phase = (up[:, None] * up[None, :] + lo[:, None] * lo[None, :]) % SIDE
    angle = 2.0 * np.pi / SIDE * phase
    table = np.stack([np.cos(angle), -np.sin(angle)]) * STRETCH
    return table.astype(ml_dtypes.bfloat16).astype(np.float32)


TABLE_SCALE = 1.0 / (STRETCH * CENTER * SIDE) ** 2


WINDOW = 112


def bin_step(values, u, l, low, acc_ref):
    n = u.shape[1]
    iota_u = lax.broadcasted_iota(jnp.int32, (WINDOW, n), 0).astype(F32).astype(BF)
    iota_l = lax.broadcasted_iota(jnp.int32, (256, n), 0).astype(F32).astype(BF)
    one, zero = jnp.ones((), BF), jnp.zeros((), BF)
    start = pl.multiple_of(jnp.minimum(low, 256 - WINDOW), 8)
    mask = iota_u == jnp.where(u >= low.astype(F32), u - start.astype(F32), -1.0).astype(BF)
    parts = [jnp.where(mask, values[c:c + 1].astype(BF), zero) for c in range(4)] + [jnp.where(mask, one, zero)]
    hot = jnp.where(iota_l == l.astype(BF), one, zero)
    sums = lax.dot_general(jnp.concatenate(parts, axis=0), hot, NTD, preferred_element_type=F32)
    for c in range(5):
        acc_ref[c, pl.ds(start, WINDOW), :] += sums[WINDOW * c:WINDOW * c + WINDOW]


def spread(pair_ref, val_ref, code_ref):
    lane = lax.broadcasted_iota(jnp.int32, (8, 128), 1)
    first, last = jnp.zeros((8, 128), F32), jnp.zeros((8, 128), F32)
    lows, highs = [None] * 3, [None] * 3
    for half in range(2):
        for g in range(8):
            at = 128 * (8 * half + g)
            vals = pair_ref[half, g, 0:48, :].astype(F32)
            codes = pair_ref[half, g, 48:72, :].astype(F32)
            for cg in range(3):
                code = codes[8 * cg:8 * cg + 8]
                val_ref[cg, :, at:at + 128] = vals[16 * cg:16 * cg + 16]
                code_ref[cg, :, at:at + 128] = code
                low = jnp.where(code < 1.0, 999.0, code)
                lows[cg] = low if lows[cg] is None else jnp.minimum(lows[cg], low)
                highs[cg] = code if highs[cg] is None else jnp.maximum(highs[cg], code)
    for cg in range(3):
        first = jnp.where(lane == cg, jnp.min(lows[cg], axis=1, keepdims=True) - 1.0, first)
        last = jnp.where(lane == cg, jnp.max(highs[cg], axis=1, keepdims=True) - 1.0, last)
    return first.astype(jnp.int32), last.astype(jnp.int32)


def split(x):
    hi = x.astype(BF)
    return hi, (x - hi.astype(F32)).astype(BF)


def quad(a, b, c, d):
    return jnp.concatenate([jnp.concatenate([a, b], axis=1), jnp.concatenate([c, d], axis=1)], axis=0)


def swap(x):
    return quad(x[:256, :256], x[256:, :256], x[:256, 256:], x[256:, 256:])


def fit(acc_ref, w_ref, tab_ref, out_ref):
    kr, ki = tab_ref[0].astype(BF), tab_ref[1].astype(BF)
    plain, conj = quad(kr, -ki, ki, kr), quad(kr, ki, -ki, kr)
    dot = functools.partial(jnp.dot, preferred_element_type=F32)

    def left(x, m):
        return dot(jnp.concatenate([m, m], axis=1), jnp.concatenate(split(x), axis=0))

    def right(x, m):
        return dot(jnp.concatenate(split(x), axis=1), jnp.concatenate([m, m], axis=0))

    def forward(x):
        return swap(right(swap(left(x, plain)), conj))

    def inverse(x):
        return swap(right(swap(left(x, conj)), plain))

    def plane(f):
        return jnp.concatenate([w_ref[pl.ds(2 * h + f, 256, stride=4), :] for h in range(2)], axis=1)

    w0, w1 = plane(0) * TABLE_SCALE, plane(1) * TABLE_SCALE
    w = quad(w0, w1, w0, w1)
    lane = lax.broadcasted_iota(jnp.int32, (1, 512), 1)

    def total(x):
        s = jnp.sum(x, axis=0, keepdims=True)
        a = jnp.sum(s[:, :256], axis=1, keepdims=True)
        b = jnp.sum(s[:, 256:], axis=1, keepdims=True)
        return jnp.where(lane < 256, a, b)

    hits = acc_ref[4]
    hits = quad(hits, hits, hits, hits)
    field = quad(acc_ref[0], acc_ref[1], acc_ref[2], acc_ref[3])
    residual = w * forward(field)
    norm = total(residual * residual)
    g0 = inverse(w * residual)
    pulled = hits * g0
    alpha = norm / (total(pulled * g0) + DAMPING * norm + EPS)
    direction = residual
    residual = residual - alpha * (w * forward(pulled) + DAMPING * direction)
    new = total(residual * residual)
    direction = residual + (new / (norm + EPS)) * direction
    g1 = inverse(w * direction)
    beta = new / (total(hits * g1 * g1) + DAMPING * total(direction * direction) + EPS)
    model = alpha * g0 + beta * g1
    for part in range(2):
        for f in range(2):
            for h in range(2):
                out_ref[part, pl.ds(2 * h + f, 256, stride=4), :] = model[
                    256 * part:256 * part + 256, 256 * f + 128 * h:256 * f + 128 * h + 128]


def solve_kernel(pair_ref, w_hbm, tab_hbm, out_ref, acc_ref, w_ref, tab_ref, val_ref, code_ref, span_vm, span_sm, sems):
    fetch = [pltpu.make_async_copy(w_hbm, w_ref, sems.at[0]), pltpu.make_async_copy(tab_hbm, tab_ref, sems.at[1])]
    for copy in fetch:
        copy.start()
    span_vm[0], span_vm[1] = spread(pair_ref, val_ref, code_ref)
    spans = pltpu.make_async_copy(span_vm, span_sm, sems.at[2])
    spans.start()
    acc_ref[...] = jnp.zeros_like(acc_ref)
    spans.wait()

    @pl.loop(0, 3)
    def _(cg):
        for i in range(4):
            first, last = span_sm[0, i, cg], span_sm[1, i, cg]
            first = (first // 8) * 8
            wide = last - first
            count = sum((wide >= WINDOW * k).astype(jnp.int32) for k in range(-(-256 // WINDOW)))

            @pl.loop(0, count)
            def _(again):
                code = code_ref[cg]
                bin_step(val_ref[cg, 4 * i:4 * i + 4, :], code[i:i + 1] - 1.0, code[4 + i:5 + i], first + again * WINDOW, acc_ref)

    for copy in fetch:
        copy.wait()
    fit(acc_ref, w_ref, tab_ref, out_ref)


MESH_ID = pl.DeviceIdType.MESH


def peer_loop(n, me, body):
    lax.fori_loop(1, n, lambda i, carry: (body(lax.rem(me + i, n)), carry)[1], 0)


def exchange_kernel(bins_ref, traces_ref, route_ref, cell_ref, out_ref,
                    traces_vm, hot_vm, bins_vm, msg_out, msg_in, pair_out,
                    trace_sem, own_sem, bin_send, bin_recv, msg_send, msg_recv, pair_send, pair_recv):
    me_p, me_f = lax.axis_index("patch"), lax.axis_index("freq")
    me_x, me_z = me_p // 8, lax.rem(me_p, 8)
    barrier = pltpu.get_barrier_semaphore()
    peer_loop(8, me_f, lambda f: pl.semaphore_signal(barrier, inc=1, device_id={"freq": f}, device_id_type=MESH_ID))
    peer_loop(32, me_p, lambda p: pl.semaphore_signal(barrier, inc=1, device_id={"patch": p}, device_id_type=MESH_ID))
    fetch = pltpu.make_async_copy(traces_ref, traces_vm, trace_sem)
    fetch.start()
    sub = lax.broadcasted_iota(jnp.int32, (8, 128), 0)
    bins_vm[me_f] = jnp.where((sub & 1) == 1, bins_ref[1], bins_ref[0])
    key, third = routing(route_ref[...], cell_ref[...])
    hot_vm[...] = one_hot_rows(key)

    def bin_copy(f, slot):
        return pltpu.make_async_remote_copy(
            src_ref=bins_vm.at[me_f], dst_ref=bins_vm.at[slot], send_sem=bin_send.at[f],
            recv_sem=bin_recv.at[slot], device_id={"freq": f}, device_id_type=MESH_ID)

    def msg_copy(p, slot):
        return pltpu.make_async_remote_copy(
            src_ref=msg_out.at[p], dst_ref=msg_in.at[slot], send_sem=msg_send.at[p],
            recv_sem=msg_recv.at[slot], device_id={"patch": p}, device_id_type=MESH_ID)

    def pair_copy(half, f, slot):
        return pltpu.make_async_remote_copy(
            src_ref=pair_out.at[half, f], dst_ref=out_ref.at[half, slot], send_sem=pair_send.at[half, f],
            recv_sem=pair_recv.at[half, slot], device_id={"freq": f}, device_id_type=MESH_ID)

    def own_copy(half):
        return pltpu.make_async_copy(pair_out.at[half, me_f], out_ref.at[half, me_f], own_sem.at[half])

    pl.semaphore_wait(barrier, 38)
    peer_loop(8, me_f, lambda f: bin_copy(f, me_f).start())
    peer_loop(8, me_f, lambda f: bin_copy(f, f).wait_recv())
    basis = make_basis(bins_vm, traces_vm.shape[1])
    fetch.wait()
    spectra = lax.dot_general(basis, traces_vm[...], NTD, preferred_element_type=F32)
    stacked = stack_rows(spectra, third, cell_ref[...])
    packed = lax.dot_general(stacked, hot_vm[...], NTD, preferred_element_type=F32)
    write_messages(packed, 8 * lax.rem(me_p, 16), msg_out)
    order = [(i // 8, i % 8) for i in range(32)]
    targets = [lax.rem(me_x + dx, 4) * 8 + lax.rem(me_z + dz, 8) for dx, dz in order]
    sources = [lax.rem(me_x + 4 - dx, 4) * 8 + lax.rem(me_z + 8 - dz, 8) for dx, dz in order]
    for p in targets[1:]:
        msg_copy(p, me_p).start()
    msg_in[me_p] = msg_out[me_p]
    for half in range(2):
        for p in sources[max(1, 16 * half):16 * half + 16]:
            msg_copy(p, p).wait_recv()
        first = lax.rem(me_x + 2 * half, 4)
        second = lax.rem(me_x + 2 * half + 3, 4)
        is_odd = lax.rem(me_x, 2)
        planes = (first + is_odd * (second - first), second + is_odd * (first - second))
        regroup(msg_in, [planes[t // 8] * 8 + t % 8 for t in range(16)], pair_out.at[half])
        peer_loop(8, me_f, lambda f: pair_copy(half, f, me_f).start())
        own_copy(half).start()
    peer_loop(8, me_f, lambda f: bin_copy(f, me_f).wait_send())
    for p in targets[1:]:
        msg_copy(p, me_p).wait_send()
    for half in range(2):
        own_copy(half).wait()
        peer_loop(8, me_f, lambda f: pair_copy(half, f, f).wait_recv())
        peer_loop(8, me_f, lambda f: pair_copy(half, f, me_f).wait_send())

def on_device(traces, routes, cells, band_bins, spectral_weight):
    rows = traces.shape[0]
    vm = pl.BlockSpec(memory_space=pltpu.VMEM)
    sm = pl.BlockSpec(memory_space=pltpu.SMEM)
    anywhere = pl.BlockSpec(memory_space=pl.ANY)
    dma = pltpu.SemaphoreType.DMA
    both = pl.pallas_call(
        exchange_kernel,
        out_shape=jax.ShapeDtypeStruct((2, 8, 72, 128), BF),
        in_specs=[sm, anywhere, vm, vm],
        out_specs=anywhere,
        scratch_shapes=[
            pltpu.VMEM(traces.shape, BF), pltpu.VMEM((1024, rows), BF), pltpu.VMEM((8, 8, 128), jnp.int32),
            pltpu.VMEM((32, 32, 128), BF), pltpu.VMEM((32, 32, 128), BF), pltpu.VMEM((2, 8, 72, 128), BF),
            dma, dma((2,)), dma((8,)), dma((8,)), dma((32,)), dma((32,)), dma((2, 8)), dma((2, 8)),
        ],
        compiler_params=pltpu.CompilerParams(
            collective_id=0, has_side_effects=True, vmem_limit_bytes=62 * 1024 * 1024),
        name="exchange",
    )(band_bins, traces, routes.reshape(1, rows), cells.reshape(1, rows))
    weight = spectral_weight.reshape(2, 512, 128).transpose(1, 0, 2).reshape(1024, 128)
    out = pl.pallas_call(
        solve_kernel,
        out_shape=jax.ShapeDtypeStruct((2, 1024, 128), F32),
        in_specs=[vm, anywhere, anywhere], out_specs=vm,
        scratch_shapes=[
            pltpu.VMEM((5, 256, 256), F32), pltpu.VMEM((1024, 128), F32), pltpu.VMEM((2, 256, 256), F32),
            pltpu.VMEM((3, 16, 2048), F32), pltpu.VMEM((3, 8, 2048), F32),
            pltpu.VMEM((2, 8, 128), jnp.int32), pltpu.SMEM((2, 8, 128), jnp.int32), dma((3,)),
        ],
        compiler_params=pltpu.CompilerParams(vmem_limit_bytes=60 * 1024 * 1024),
        name="solve",
    )(both, weight, jnp.asarray(kernel_table()))
    return out.reshape(2, 512, 2, 128).transpose(0, 2, 1, 3).reshape(2, 2, 65536)


def solution(mesh):
    return jax.shard_map(
        on_device,
        mesh=mesh,
        in_specs=(P(("patch", "freq"), None), P(("patch", "freq"), None), P(("patch", "freq")), P("freq"), P("freq", "patch")),
        out_specs=P(None, "freq", "patch"),
        check_vma=False,
    )
```

time: 69.8 us -> 53.5 us (0.77)
  Pallas kernels: 64.7 us -> 52.8 us
  local copies, waits for them, and re-layouts: 4.92 us -> 0 us
    pallas_call x1, Pallas kernels: 31.7 us -> 20.4 us  [on_device(): pl.pallas_call(solve_kernel, out_shape=jax.ShapeDtypeStruct((2, 1024, 128...]
    unnamed x10 -> x0, local copies, waits for them, and re-layouts: 4.92 us -> none
where the time goes in v3:
time: 53.5 us; the launch traced here: 52.8 us
  Pallas kernels  52.8 us (99%)
    pallas_call x1, Pallas kernels, on_device(): pl.pallas_call(exchange_kernel, out_shape=jax.ShapeDtypeStruct((2, 8, 72,...  32.4 us
    pallas_call x1, Pallas kernels, on_device(): pl.pallas_call(solve_kernel, out_shape=jax.ShapeDtypeStruct((2, 1024, 128...  20.4 us

profile of v3, /device:TPU:1, one launch (start us, length us, event | category | flops | bytes accessed | tf_op | source)
XLA Modules:
  0.0 52.8 jit_solution(18407773685724989408)
XLA Ops:
  0.0 32.4 %exchange.1.pair_ref = bf16[2,8,72,128]{3,2,1,0:T(8,128)(2,1)} custom-call(s32[2]{0:T(128)} %bins_ref.1, bf16[1024,2048]{1,0:T(8,128)(2,1)} %traces_ref.1, s32[1,1024]{1,0:T(1,128)} %bitcast.13, s32[1,1024]{1,0:T(1,128)} %bitcast.14), custom_call_target="tpu_custom_call" | custom-call | tf_op jit(solution)/shard_map/exchange/pallas_call | solution.py:342
  32.4 20.4 %solve.1 = f32[2,1024,128]{2,1,0:T(8,128)} custom-call(bf16[2,8,72,128]{3,2,1,0:T(8,128)(2,1)} %exchange.1.pair_ref, f32[1024,128]{1,0:T(8,128)} %bitcast.12, f32[2,256,256]{2,1,0:T(8,128)} %constant.2.clone.tab_hbm), custom_call_target="tpu_custom_call" | custom-call | tf_op jit(solution)/shard_map/solve/pallas_call | solution.py:357

commit v4 on v3

--- a/solution.py
+++ b/solution.py
@@ -6,7 +6,9 @@
 from jax import lax
 from jax.experimental import pallas as pl
 from jax.experimental.pallas import tpu as pltpu
-F32=jnp.float32; BF=jnp.bfloat16
+F32 = jnp.float32
+BF = jnp.bfloat16
+CAP = 96
 NTD=(((1,),(1,)),((),()))
 
 
@@ -31,20 +33,36 @@
     phase = (kk * t + pp) & (nt - 1)
     return (cosine(phase, nt) * (1.0 / math.sqrt(nt))).astype(BF)
 
+def columns_of(row):
+    return [jnp.broadcast_to(row[:, a:a + 128], (128, 128)).T for a in range(0, row.shape[1], 128)]
+
+
 def routing(route, cell):
     rows = route.shape[1]
     key = (route << 26) + (cell << 10) + lax.broadcasted_iota(jnp.int32, (1, rows), 1)
+    key_columns = columns_of(key)
     smaller = jnp.zeros((8, rows), F32)
-    for a in range(rows // 128):
-        column = jnp.broadcast_to(key[:, 128 * a:128 * a + 128], (128, 128)).T
+    for column in key_columns:
         for i in range(16):
             part = jnp.concatenate([column[8 * i:8 * i + 8]] * (rows // 128), axis=1)
             smaller = smaller + jnp.where(part < key, 1.0, 0.0)
     patch = lax.broadcasted_iota(jnp.int32, (32, rows), 0)
+    member = route == patch
     before = jnp.sum(jnp.where(route < patch, 1.0, 0.0), axis=1, keepdims=True)
-    rank = jnp.sum(smaller, axis=0, keepdims=True) - jnp.sum(jnp.where(route == patch, before, 0.0), axis=0, keepdims=True)
-    rank = rank.astype(jnp.int32)
-    return route * 32 + (rank & 31), rank >> 5
+    room = CAP - jnp.sum(jnp.where(member, 1.0, 0.0), axis=1, keepdims=True)
+    rank = jnp.sum(smaller, axis=0, keepdims=True) - jnp.sum(jnp.where(member, before, 0.0), axis=0, keepdims=True)
+    room = jnp.sum(jnp.where(member, room, 0.0), axis=0, keepdims=True)
+    base = (route << 8).astype(F32)
+    ahead = base + ((cell * 3) >> 11).astype(F32) - rank
+    most = jnp.full((8, rows), -1000.0, F32)
+    for column, lead in zip(key_columns, columns_of(ahead)):
+        for i in range(16):
+            part = jnp.concatenate([column[8 * i:8 * i + 8]] * (rows // 128), axis=1)
+            value = jnp.concatenate([lead[8 * i:8 * i + 8]] * (rows // 128), axis=1)
+            most = jnp.where(part <= key, jnp.maximum(most, value), most)
+    slot = (rank + jnp.minimum(jnp.max(most, axis=0, keepdims=True) - base, room)).astype(jnp.int32)
+    return route * 32 + (slot & 31), slot >> 5
+
 
 def stack_rows(spectra, third, cell):
     rows = spectra.shape[1]
@@ -60,10 +78,10 @@
     rows = key.shape[1]
     return jnp.where(lax.broadcasted_iota(jnp.int32, (1024, rows), 0) == key, 1.0, 0.0).astype(BF)
 
-def write_messages(packed, turn, msg_ref):
+def write_messages(packed, turn, first, msg_ref):
     lane = lax.broadcasted_iota(jnp.int32, (32, 128), 1) >> 5
-    for cb in range(8):
-        groups = [packed[32*g:32*g+32, 128*cb:128*cb+128] for g in range(4)]
+    for cb in range(2):
+        groups = [packed[32 * g:32 * g + 32, 128 * cb:128 * cb + 128] for g in range(4)]
         for pm in range(4):
             out = jnp.zeros((32, 128), F32)
             for g in range(4):
@@ -72,7 +90,8 @@
                 if shift:
                     piece = pltpu.roll(piece, shift, 1)
                 out = jnp.where(lane == g, piece, out)
-            msg_ref[4*cb+pm] = pltpu.roll(out, turn, 1).astype(BF)
+            msg_ref[first + 4 * cb + pm] = pltpu.roll(out, turn, 1).astype(BF)
+
 
 def regroup(msg_ref, sources, pair_ref):
     lane = lax.broadcasted_iota(jnp.int32, (32, 128), 1) >> 3
@@ -279,8 +298,6 @@
     fetch.start()
     sub = lax.broadcasted_iota(jnp.int32, (8, 128), 0)
     bins_vm[me_f] = jnp.where((sub & 1) == 1, bins_ref[1], bins_ref[0])
-    key, third = routing(route_ref[...], cell_ref[...])
-    hot_vm[...] = one_hot_rows(key)
 
     def bin_copy(f, slot):
         return pltpu.make_async_remote_copy(
@@ -302,18 +319,22 @@
 
     pl.semaphore_wait(barrier, 38)
     peer_loop(8, me_f, lambda f: bin_copy(f, me_f).start())
+    key, third = routing(route_ref[...], cell_ref[...])
+    hot_vm[...] = one_hot_rows(key)
     peer_loop(8, me_f, lambda f: bin_copy(f, f).wait_recv())
     basis = make_basis(bins_vm, traces_vm.shape[1])
     fetch.wait()
     spectra = lax.dot_general(basis, traces_vm[...], NTD, preferred_element_type=F32)
     stacked = stack_rows(spectra, third, cell_ref[...])
-    packed = lax.dot_general(stacked, hot_vm[...], NTD, preferred_element_type=F32)
-    write_messages(packed, 8 * lax.rem(me_p, 16), msg_out)
     order = [(i // 8, i % 8) for i in range(32)]
     targets = [lax.rem(me_x + dx, 4) * 8 + lax.rem(me_z + dz, 8) for dx, dz in order]
     sources = [lax.rem(me_x + 4 - dx, 4) * 8 + lax.rem(me_z + 8 - dz, 8) for dx, dz in order]
-    for p in targets[1:]:
-        msg_copy(p, me_p).start()
+    for dx in range(4):
+        plane = lax.rem(me_x + dx, 4)
+        packed = lax.dot_general(stacked, hot_vm[pl.ds(pl.multiple_of(256 * plane, 256), 256), :], NTD, preferred_element_type=F32)
+        write_messages(packed, 8 * lax.rem(me_p, 16), 8 * plane, msg_out)
+        for p in targets[max(1, 8 * dx):8 * dx + 8]:
+            msg_copy(p, me_p).start()
     msg_in[me_p] = msg_out[me_p]
     for half in range(2):
         for p in sources[max(1, 16 * half):16 * half + 16]:

time: 53.5 us -> 50.5 us (0.944); the launches traced: 52.8 us -> 50.4 us
  Pallas kernels: 52.8 us -> 50.2 us
    pallas_call x1, Pallas kernels: 20.4 us -> 18.2 us  [on_device(): pl.pallas_call(solve_kernel, out_shape=jax.ShapeDtypeStruct((2, 1024, 128...]
where the time goes in v4:
time: 50.5 us; the launch traced here: 50.4 us
  Pallas kernels  50.2 us (99%)
    pallas_call x1, Pallas kernels, on_device(): pl.pallas_call(exchange_kernel, out_shape=jax.ShapeDtypeStruct((2, 8, 72,...  32 us
    pallas_call x1, Pallas kernels, on_device(): pl.pallas_call(solve_kernel, out_shape=jax.ShapeDtypeStruct((2, 1024, 128...  18.2 us

profile of v4, /device:TPU:1, one launch (start us, length us, event | category | flops | bytes accessed | tf_op | source)
XLA Modules:
  0.0 50.4 jit_solution(5368085425619706298)
XLA Ops:
  0.0 32.0 %exchange.1.pair_ref = bf16[2,8,72,128]{3,2,1,0:T(8,128)(2,1)} custom-call(s32[2]{0:T(128)} %bins_ref.1, bf16[1024,2048]{1,0:T(8,128)(2,1)} %traces_ref.1, s32[1,1024]{1,0:T(1,128)} %bitcast.13, s32[1,1024]{1,0:T(1,128)} %bitcast.14), custom_call_target="tpu_custom_call" | custom-call | tf_op jit(solution)/shard_map/exchange/pallas_call | solution.py:363
  32.0 18.2 %solve.1 = f32[2,1024,128]{2,1,0:T(8,128)} custom-call(bf16[2,8,72,128]{3,2,1,0:T(8,128)(2,1)} %exchange.1.pair_ref, f32[1024,128]{1,0:T(8,128)} %bitcast.12, f32[2,256,256]{2,1,0:T(8,128)} %constant.2.clone.tab_hbm), custom_call_target="tpu_custom_call" | custom-call | tf_op jit(solution)/shard_map/solve/pallas_call | solution.py:378

commit v5 on v4

--- a/solution.py
+++ b/solution.py
@@ -148,20 +148,21 @@
 
 
 WINDOW = 112
-
-
-def bin_step(values, u, l, low, acc_ref):
+USUAL = ((64, 88, 96, 112), (112, 120, 112, 112), (104, 96, 80, 64))
+
+
+def bin_step(values, u, l, low, window, acc_ref):
     n = u.shape[1]
-    iota_u = lax.broadcasted_iota(jnp.int32, (WINDOW, n), 0).astype(F32).astype(BF)
+    iota_u = lax.broadcasted_iota(jnp.int32, (window, n), 0).astype(F32).astype(BF)
     iota_l = lax.broadcasted_iota(jnp.int32, (256, n), 0).astype(F32).astype(BF)
     one, zero = jnp.ones((), BF), jnp.zeros((), BF)
-    start = pl.multiple_of(jnp.minimum(low, 256 - WINDOW), 8)
+    start = pl.multiple_of(jnp.minimum(low, 256 - window), 8)
     mask = iota_u == jnp.where(u >= low.astype(F32), u - start.astype(F32), -1.0).astype(BF)
     parts = [jnp.where(mask, values[c:c + 1].astype(BF), zero) for c in range(4)] + [jnp.where(mask, one, zero)]
     hot = jnp.where(iota_l == l.astype(BF), one, zero)
     sums = lax.dot_general(jnp.concatenate(parts, axis=0), hot, NTD, preferred_element_type=F32)
     for c in range(5):
-        acc_ref[c, pl.ds(start, WINDOW), :] += sums[WINDOW * c:WINDOW * c + WINDOW]
+        acc_ref[c, pl.ds(start, window), :] += sums[window * c:window * c + window]
 
 
 def spread(pair_ref, val_ref, code_ref):
@@ -241,7 +242,7 @@
     residual = residual - alpha * (w * forward(pulled) + DAMPING * direction)
     new = total(residual * residual)
     direction = residual + (new / (norm + EPS)) * direction
-    g1 = inverse(w * direction)
+    g1 = swap(dot(swap(dot(conj, (w * direction).astype(BF))).astype(BF), plain))
     beta = new / (total(hits * g1 * g1) + DAMPING * total(direction * direction) + EPS)
     model = alpha * g0 + beta * g1
     for part in range(2):
@@ -261,18 +262,28 @@
     acc_ref[...] = jnp.zeros_like(acc_ref)
     spans.wait()
 
-    @pl.loop(0, 3)
-    def _(cg):
+    for cg in range(3):
+        steps, usual = [], True
         for i in range(4):
             first, last = span_sm[0, i, cg], span_sm[1, i, cg]
-            first = (first // 8) * 8
+            first = jnp.minimum((first // 8) * 8, 248)
             wide = last - first
-            count = sum((wide >= WINDOW * k).astype(jnp.int32) for k in range(-(-256 // WINDOW)))
-
-            @pl.loop(0, count)
-            def _(again):
-                code = code_ref[cg]
-                bin_step(val_ref[cg, 4 * i:4 * i + 4, :], code[i:i + 1] - 1.0, code[4 + i:5 + i], first + again * WINDOW, acc_ref)
+            usual = jnp.logical_and(usual, wide < USUAL[cg][i])
+            steps.append((first, sum((wide >= WINDOW * k).astype(jnp.int32) for k in range(-(-256 // WINDOW)))))
+
+        def add(i, low, window):
+            code = code_ref[cg]
+            bin_step(val_ref[cg, 4 * i:4 * i + 4, :], code[i:i + 1] - 1.0, code[4 + i:5 + i], low, window, acc_ref)
+
+        @pl.when(usual)
+        def _():
+            for i in range(4):
+                add(i, steps[i][0], USUAL[cg][i])
+
+        @pl.when(jnp.logical_not(usual))
+        def _():
+            for i in range(4):
+                pl.loop(0, steps[i][1])(lambda again: add(i, steps[i][0] + again * WINDOW, WINDOW))
 
     for copy in fetch:
         copy.wait()

time: 50.5 us -> 47.2 us (0.935)
  Pallas kernels: 50.2 us -> 46.9 us
    pallas_call x1, Pallas kernels: 18.2 us -> 14.9 us  [on_device(): pl.pallas_call(solve_kernel, out_shape=jax.ShapeDtypeStruct((2, 1024, 128...]
where the time goes in v5:
time: 47.2 us; the launch traced here: 47.1 us
  Pallas kernels  46.9 us (99%)
    pallas_call x1, Pallas kernels, on_device(): pl.pallas_call(exchange_kernel, out_shape=jax.ShapeDtypeStruct((2, 8, 72,...  32 us
    pallas_call x1, Pallas kernels, on_device(): pl.pallas_call(solve_kernel, out_shape=jax.ShapeDtypeStruct((2, 1024, 128...  14.9 us

profile of v5, /device:TPU:1, one launch (start us, length us, event | category | flops | bytes accessed | tf_op | source)
XLA Modules:
  0.0 47.1 jit_solution(4715430205353060710)
XLA Ops:
  0.0 32.0 %exchange.1.pair_ref = bf16[2,8,72,128]{3,2,1,0:T(8,128)(2,1)} custom-call(s32[2]{0:T(128)} %bins_ref.1, bf16[1024,2048]{1,0:T(8,128)(2,1)} %traces_ref.1, s32[1,1024]{1,0:T(1,128)} %bitcast.13, s32[1,1024]{1,0:T(1,128)} %bitcast.14), custom_call_target="tpu_custom_call" | custom-call | tf_op jit(solution)/shard_map/exchange/pallas_call | solution.py:374
  32.0 14.9 %solve.1 = f32[2,1024,128]{2,1,0:T(8,128)} custom-call(bf16[2,8,72,128]{3,2,1,0:T(8,128)(2,1)} %exchange.1.pair_ref, f32[1024,128]{1,0:T(8,128)} %bitcast.12, f32[2,256,256]{2,1,0:T(8,128)} %constant.2.clone.tab_hbm), custom_call_target="tpu_custom_call" | custom-call | tf_op jit(solution)/shard_map/solve/pallas_call | solution.py:389

commit v6 on v5

--- a/solution.py
+++ b/solution.py
@@ -200,7 +200,7 @@
     return quad(x[:256, :256], x[256:, :256], x[:256, 256:], x[256:, 256:])
 
 
-def fit(acc_ref, w_ref, tab_ref, out_ref):
+def fit(acc_ref, w_ref, tab_ref, out_hbm, out_ref, out_sem):
     kr, ki = tab_ref[0].astype(BF), tab_ref[1].astype(BF)
     plain, conj = quad(kr, -ki, ki, kr), quad(kr, ki, -ki, kr)
     dot = functools.partial(jnp.dot, preferred_element_type=F32)
@@ -233,7 +233,7 @@
     hits = acc_ref[4]
     hits = quad(hits, hits, hits, hits)
     field = quad(acc_ref[0], acc_ref[1], acc_ref[2], acc_ref[3])
-    residual = w * forward(field)
+    residual = w * swap(right(swap(dot(plain, field.astype(BF))), conj))
     norm = total(residual * residual)
     g0 = inverse(w * residual)
     pulled = hits * g0
@@ -244,15 +244,21 @@
     direction = residual + (new / (norm + EPS)) * direction
     g1 = swap(dot(swap(dot(conj, (w * direction).astype(BF))).astype(BF), plain))
     beta = new / (total(hits * g1 * g1) + DAMPING * total(direction * direction) + EPS)
-    model = alpha * g0 + beta * g1
+    stores = [pltpu.make_async_copy(out_ref.at[part], out_hbm.at[part], out_sem.at[part]) for part in range(2)]
     for part in range(2):
+        rows = slice(256 * part, 256 * part + 256)
+        model = alpha * g0[rows] + beta * g1[rows]
         for f in range(2):
             for h in range(2):
-                out_ref[part, pl.ds(2 * h + f, 256, stride=4), :] = model[
-                    256 * part:256 * part + 256, 256 * f + 128 * h:256 * f + 128 * h + 128]
-
-
-def solve_kernel(pair_ref, w_hbm, tab_hbm, out_ref, acc_ref, w_ref, tab_ref, val_ref, code_ref, span_vm, span_sm, sems):
+                at = 256 * f + 128 * h
+                out_ref[part, pl.ds(2 * h + f, 256, stride=4), :] = model[:, at:at + 128]
+        stores[part].start()
+    for store in stores:
+        store.wait()
+
+
+def solve_kernel(pair_ref, w_hbm, tab_hbm, out_hbm, out_ref, acc_ref, w_ref, tab_ref, val_ref, code_ref, span_vm, span_sm, sems,
+                 out_sem):
     fetch = [pltpu.make_async_copy(w_hbm, w_ref, sems.at[0]), pltpu.make_async_copy(tab_hbm, tab_ref, sems.at[1])]
     for copy in fetch:
         copy.start()
@@ -287,7 +293,7 @@
 
     for copy in fetch:
         copy.wait()
-    fit(acc_ref, w_ref, tab_ref, out_ref)
+    fit(acc_ref, w_ref, tab_ref, out_hbm, out_ref, out_sem)
 
 
 MESH_ID = pl.DeviceIdType.MESH
@@ -337,29 +343,31 @@
     fetch.wait()
     spectra = lax.dot_general(basis, traces_vm[...], NTD, preferred_element_type=F32)
     stacked = stack_rows(spectra, third, cell_ref[...])
-    order = [(i // 8, i % 8) for i in range(32)]
+    order = [(dx, dz) for dx in (1, 2, 3, 0) for dz in (4, 3, 5, 2, 6, 1, 7, 0)]
     targets = [lax.rem(me_x + dx, 4) * 8 + lax.rem(me_z + dz, 8) for dx, dz in order]
     sources = [lax.rem(me_x + 4 - dx, 4) * 8 + lax.rem(me_z + 8 - dz, 8) for dx, dz in order]
-    for dx in range(4):
-        plane = lax.rem(me_x + dx, 4)
+    for k in range(4):
+        plane = lax.rem(me_x + order[8 * k][0], 4)
         packed = lax.dot_general(stacked, hot_vm[pl.ds(pl.multiple_of(256 * plane, 256), 256), :], NTD, preferred_element_type=F32)
         write_messages(packed, 8 * lax.rem(me_p, 16), 8 * plane, msg_out)
-        for p in targets[max(1, 8 * dx):8 * dx + 8]:
-            msg_copy(p, me_p).start()
+        for p in [i for i in range(8 * k, 8 * k + 8) if order[i] != (0, 0)]:
+            msg_copy(targets[p], me_p).start()
     msg_in[me_p] = msg_out[me_p]
     for half in range(2):
-        for p in sources[max(1, 16 * half):16 * half + 16]:
-            msg_copy(p, p).wait_recv()
-        first = lax.rem(me_x + 2 * half, 4)
-        second = lax.rem(me_x + 2 * half + 3, 4)
-        is_odd = lax.rem(me_x, 2)
+        for i in range(16 * half, 16 * half + 16):
+            if order[i] != (0, 0):
+                msg_copy(sources[i], sources[i]).wait_recv()
+        first = lax.rem(me_x + 4 - order[16 * half][0], 4)
+        second = lax.rem(me_x + 4 - order[16 * half + 8][0], 4)
+        is_odd = lax.rem(first, 2)
         planes = (first + is_odd * (second - first), second + is_odd * (first - second))
         regroup(msg_in, [planes[t // 8] * 8 + t % 8 for t in range(16)], pair_out.at[half])
         peer_loop(8, me_f, lambda f: pair_copy(half, f, me_f).start())
         own_copy(half).start()
     peer_loop(8, me_f, lambda f: bin_copy(f, me_f).wait_send())
-    for p in targets[1:]:
-        msg_copy(p, me_p).wait_send()
+    for i in range(32):
+        if order[i] != (0, 0):
+            msg_copy(targets[i], me_p).wait_send()
     for half in range(2):
         own_copy(half).wait()
         peer_loop(8, me_f, lambda f: pair_copy(half, f, f).wait_recv())
@@ -389,11 +397,11 @@
     out = pl.pallas_call(
         solve_kernel,
         out_shape=jax.ShapeDtypeStruct((2, 1024, 128), F32),
-        in_specs=[vm, anywhere, anywhere], out_specs=vm,
+        in_specs=[vm, anywhere, anywhere], out_specs=anywhere,
         scratch_shapes=[
-            pltpu.VMEM((5, 256, 256), F32), pltpu.VMEM((1024, 128), F32), pltpu.VMEM((2, 256, 256), F32),
+            pltpu.VMEM((2, 1024, 128), F32), pltpu.VMEM((5, 256, 256), F32), pltpu.VMEM((1024, 128), F32), pltpu.VMEM((2, 256, 256), F32),
             pltpu.VMEM((3, 16, 2048), F32), pltpu.VMEM((3, 8, 2048), F32),
-            pltpu.VMEM((2, 8, 128), jnp.int32), pltpu.SMEM((2, 8, 128), jnp.int32), dma((3,)),
+            pltpu.VMEM((2, 8, 128), jnp.int32), pltpu.SMEM((2, 8, 128), jnp.int32), dma((3,)), dma((2,)),
         ],
         compiler_params=pltpu.CompilerParams(vmem_limit_bytes=60 * 1024 * 1024),
         name="solve",

time: 47.2 us -> 46.9 us (level)
  no operation moved by 1% of the time
where the time goes in v6:
time: 46.9 us; the launch traced here: 46.7 us
  Pallas kernels  46.6 us (99%)
    pallas_call x1, Pallas kernels, on_device(): pl.pallas_call(exchange_kernel, out_shape=jax.ShapeDtypeStruct((2, 8, 72,...  32 us
    pallas_call x1, Pallas kernels, on_device(): pl.pallas_call(solve_kernel, out_shape=jax.ShapeDtypeStruct((2, 1024, 128...  14.6 us

profile of v6, /device:TPU:1, one launch (start us, length us, event | category | flops | bytes accessed | tf_op | source)
XLA Modules:
  0.0 46.7 jit_solution(4729637867177130191)
XLA Ops:
  0.0 32.0 %exchange.1.pair_ref = bf16[2,8,72,128]{3,2,1,0:T(8,128)(2,1)} custom-call(s32[2]{0:T(128)} %bins_ref.1, bf16[1024,2048]{1,0:T(8,128)(2,1)} %traces_ref.1, s32[1,1024]{1,0:T(1,128)} %bitcast.13, s32[1,1024]{1,0:T(1,128)} %bitcast.14), custom_call_target="tpu_custom_call" | custom-call | tf_op jit(solution)/shard_map/exchange/pallas_call | solution.py:382
  32.0 14.6 %solve.1 = f32[2,1024,128]{2,1,0:T(8,128)} custom-call(bf16[2,8,72,128]{3,2,1,0:T(8,128)(2,1)} %exchange.1.pair_ref, f32[1024,128]{1,0:T(8,128)} %bitcast.12, f32[2,256,256]{2,1,0:T(8,128)} %constant.2.clone.tab_hbm), custom_call_target="tpu_custom_call" | custom-call | tf_op jit(solution)/shard_map/solve/pallas_call | solution.py:397
